TPU v7x, 512 devices: a whole 4x8x8 slice. The times are simulated.
512 devices in a mesh: row: 32 (over y, x), col: 16 (over z, core).
Axes of the slice: x: 4, y: 8, z: 8, core: 2. Of those that a mesh axis runs over, the one named last changes fastest.
Arguments:
- choi: float32 [4, 8192, 4096], P(None, 'row', 'col'), may hold values from -0.5 to 8, as said below
Outputs:
- factored: float32 [4, 8192, 4096], P(None, 'row', 'col')
Inputs may be any that keep to these rules, and one draw needn't show every extreme that they name: `choi`: the leading 4096 x 4096 block of the matrix is symmetric with a positive diagonal, and its leading 2 * 256 square is positive definite.
All inputs are finite; a program needn't handle non-finite values.
Results may differ from a plain program's by a relative error of at most 0.0001.
Values sent between devices are 32-bit elements; how exact they have to be, the bound alone decides.
No kernel may reach another device: no remote copies, remote signals or barrier semaphores. Data moves between devices by JAX's collectives and lax.ppermute only.
A program may use at most 64 MiB of HBM per device.

v0:
```python
import jax
import jax.numpy as jnp
from jax import lax
from jax.experimental import pallas as pl
from jax.experimental.pallas import tpu as pltpu
from jax.sharding import Mesh
from jax.sharding import PartitionSpec as P

PANELS = 2
HIGHEST = lax.Precision.HIGHEST
STEPS = 40
LAST = 5e-4
ROW = ("y", "x")
COL = ("z", "core")


def doubling(block, axis, size):
    place = lax.axis_index(axis)
    step = size // 2
    while step:
        pairs = [(i, i + step) for i in range(0, size, 2 * step)]
        sent = lax.ppermute(block, axis, pairs)
        block = jnp.where(place % (2 * step) == step, sent, block)
        step //= 2
    return block


def panels_of(choi):
    slots, tile, _ = choi.shape
    deep = lax.axis_size("z")
    flat = choi.reshape(deep, slots * tile // deep, tile)
    piece = jnp.where(lax.axis_index("z") == 0, flat[0], 0.0)
    for z in range(1, deep):
        piece = piece + lax.ppermute(flat[z], "z", [(0, z)])
    whole = lax.all_gather(piece, COL)
    whole = whole.reshape(deep, 2, *piece.shape)
    return jnp.concatenate(
        [whole[:, k].reshape(slots * tile, tile) for k in range(PANELS)], axis=1
    )


def top_rows(choi):
    tile = choi.shape[1]
    high = lax.axis_size("y")
    x = lax.axis_index("x")
    core = lax.axis_index("core")
    part = tile // high
    mine = lax.all_to_all(choi[0].reshape(high, part, tile), "y", 0, 0)[0]
    other = lax.ppermute(mine, "x", [(0, 1), (1, 0)])
    both = jnp.where(x == 0, jnp.concatenate([mine, other]), jnp.concatenate([other, mine]))
    both = jnp.where(x < 2, both, lax.ppermute(both, "x", [(0, 3), (1, 2)]))
    lead = doubling(both, "z", lax.axis_size("z"))
    sent = jnp.concatenate([both, lead])
    got = lax.all_to_all(jnp.broadcast_to(sent, (high, *sent.shape)), "y", 0, 0)
    got = got.reshape(high, 4, part, tile).transpose(1, 0, 2, 3).reshape(2, 2 * tile, tile)
    column, half = got[0], got[1]
    pair = lax.ppermute(half, "core", [(0, 1), (1, 0)])
    lead = jnp.where(
        core == 0,
        jnp.concatenate([half, pair], axis=1),
        jnp.concatenate([pair, half], axis=1),
    )
    return column, lead


def product(left, right, contract=((1,), (0,)), precision=HIGHEST):
    return lax.dot_general(
        left, right, (contract, ((), ())), precision=precision,
        preferred_element_type=jnp.float32,
    )


def square(block):
    return jnp.sum(block * block)


def eliminate(lead_ref, inverse_ref, work_ref):
    order = lead_ref.shape[0]
    rows = lax.broadcasted_iota(jnp.int32, (order, order), 0)
    cols = lax.broadcasted_iota(jnp.int32, (order, order), 1)
    work_ref[...] = lead_ref[...]
    inverse_ref[...] = (rows == cols).astype(jnp.float32)

    def pivot(k, carry):
        work = work_ref[...]
        column = jnp.sum(jnp.where(cols == k, work, 0.0), axis=1, keepdims=True)
        place = lax.broadcasted_iota(jnp.int32, (order, 1), 0)
        corner = jnp.sum(jnp.where(place == k, column, 0.0))
        scale = jnp.full((order, 1), corner)
        ratio = jnp.where(place > k, column / scale, 0.0)
        work_ref[...] = work - ratio * work_ref[pl.ds(k, 1), :]
        inverse = inverse_ref[...] - ratio * inverse_ref[pl.ds(k, 1), :]
        inverse_ref[...] = jnp.where(place == k, inverse / jnp.sqrt(scale), inverse)
        return carry

    lax.fori_loop(0, order, pivot, 0)


def factor_kernel(lead_ref, inverse_ref, factor_ref, work_ref):
    order = lead_ref.shape[0]
    half = order // 2
    rows = lax.broadcasted_iota(jnp.int32, (order, order), 0)
    cols = lax.broadcasted_iota(jnp.int32, (order, order), 1)
    same = rows == cols
    lead = lead_ref[...]
    down = lax.rsqrt(jnp.sum(jnp.where(same, lead, 0.0), axis=1, keepdims=True))
    along = lax.rsqrt(jnp.sum(jnp.where(same, lead, 0.0), axis=0, keepdims=True))
    scaled = lead * down * along
    off = jnp.where(same, 0.0, scaled).astype(jnp.bfloat16)
    twice = product(off, off, precision=None)
    bound = jnp.sqrt(jnp.sqrt(jnp.full((1, 1), square(twice))))
    shrink = jnp.where(bound < 1.0, jnp.ones_like(bound), 1.0 / (1.0 + bound))
    first = jnp.where(rows > cols, -scaled * shrink, jnp.where(same, 1.5 - 0.5 * shrink, 0.0))
    inverse_ref[...] = first * along * jnp.sqrt(shrink)

    top, low = pl.ds(0, half), pl.ds(half, half)
    small_rows = rows[:half, :half]
    small_cols = cols[:half, :half]
    unit = (small_rows == small_cols).astype(jnp.float32)
    across = ((1,), (1,))

    def lower(block):
        return jnp.where(small_rows > small_cols, block, 0.5 * unit * block)

    def unfinished(carry):
        count, residual = carry
        return (count < STEPS) & (residual > LAST)

    def newton(carry):
        count, _ = carry
        x00, x10, x11 = inverse_ref[top, top], inverse_ref[low, top], inverse_ref[low, low]
        s00, s10 = lead_ref[top, top], lead_ref[low, top]
        s01, s11 = lead_ref[top, low], lead_ref[low, low]
        y00 = product(x00, s00)
        y10 = product(x10, s00) + product(x11, s10)
        y11 = product(x10, s01) + product(x11, s11)
        e00 = product(y00, x00, across) - unit
        e10 = product(y10, x00, across)
        e11 = product(y10, x10, across) + product(y11, x11, across) - unit
        residual = jnp.sqrt(square(e00) + 2.0 * square(e10) + square(e11))
        f00, f11 = lower(e00), lower(e11)
        inverse_ref[top, top] = x00 - product(f00, x00)
        inverse_ref[low, top] = x10 - product(e10, x00) - product(f11, x10)
        inverse_ref[low, low] = x11 - product(f11, x11)
        return count + 1, residual

    _, residual = lax.while_loop(unfinished, newton, (jnp.int32(0), jnp.float32(1.0)))

    @pl.when(jnp.logical_not(residual <= LAST))
    def _():
        eliminate(lead_ref, inverse_ref, work_ref)

    factor = product(lead_ref[...], inverse_ref[...], across)
    factor_ref[...] = jnp.where(rows >= cols, factor, 0.0)


def factor_of(lead):
    shape = jax.ShapeDtypeStruct(lead.shape, jnp.float32)
    inverse, factor = pl.pallas_call(
        factor_kernel,
        out_shape=(shape, shape),
        scratch_shapes=[pltpu.VMEM(lead.shape, jnp.float32)],
        compiler_params=pltpu.CompilerParams(vmem_limit_bytes=40 * 2**20),
        cost_estimate=pl.CostEstimate(
            flops=20 * lead.shape[0] ** 3, bytes_accessed=12 * lead.size, transcendentals=0
        ),
    )(lead)
    return factor, inverse


def body(choi):
    slots, tile, _ = choi.shape
    row = lax.axis_index(ROW)
    col = lax.axis_index(COL)
    panels = panels_of(choi)
    column, lead = top_rows(choi)
    factor, inverse = factor_of(lead)
    in_panel = col < PANELS
    half = jnp.dot(inverse, column, precision=HIGHEST)
    identity = jnp.eye(2 * tile, dtype=jnp.float32)
    place = jnp.minimum(col, PANELS - 1) * tile
    chosen = lax.dynamic_slice(identity, (0, place), (2 * tile, tile))
    half = jnp.where(in_panel, -chosen, half)
    weight = lax.dot_general(
        inverse, half, (((0,), (0,)), ((), ())), precision=HIGHEST
    )
    base = jnp.where(in_panel, 0.0, choi)
    change = jnp.dot(panels, weight, precision=HIGHEST).reshape(choi.shape)
    result = base - change
    corner = lax.dynamic_slice(
        factor, (jnp.minimum(row, PANELS - 1) * tile, place), (tile, tile)
    )
    corner = jnp.where(in_panel, corner, 0.0)
    slot = jnp.arange(slots)[:, None, None]
    return jnp.where((slot == 0) & (row < PANELS), corner[None], result)


def solution(mesh):
    finer = Mesh(mesh.devices.reshape(8, 4, 8, 2), ("y", "x", "z", "core"))
    spec = P(None, ROW, COL)
    return jax.shard_map(
        body, mesh=finer, in_specs=(spec,), out_specs=spec, check_vma=False
    )
```

profile of v0, /device:TPU:1, one launch (start us, length us, event | category | flops | bytes accessed | tf_op | source)
XLA Modules:
  0.0 129.2 jit_solution(4038011124334311927)
XLA Ops:
  6.5 1.1 slice.44
  7.6 16.7 %all_to_all.10 = f32[8,32,256]{2,1,0:T(8,128)S(1)} all-to-all(f32[8,32,256]{2,1,0:T(8,128)S(1)} %bitcast.58), channel_id=1, replica_groups=mesh['y'=8,'x'=4,'z'=8,'core'=2] {'y'}, dimensions={0} | all-to-all | bytes 524288 | tf_op jit(solution)/shard_map/all_to_all | solution.py:48
  24.3 4.2 %collective-permute-start = (f32[32,256]{1,0:T(8,128)S(1)}, f32[32,256]{1,0:T(8,128)S(1)}, u32[]{:S(2)}, u32[]{:S(2)}) collective-permute-start(f32[32,256]{1,0:T(8,128)S(1)} %slice_bitcast_fusion.7), channel_id=1, source_target_pairs={{0,16},{16,0},{1,17},{17,1},{2,18},{18,2},{3,19},{19,3},{4,20},{20... | collective-permute-start | bytes 98312 | tf_op jit(solution)/shard_map/ppermute | solution.py:49
  28.5 1.3 collective-permute-done
  29.8 1.3 %collective-permute-start.1 = (f32[64,256]{1,0:T(8,128)S(1)}, f32[64,256]{1,0:T(8,128)S(1)}, u32[]{:S(2)}, u32[]{:S(2)}) collective-permute-start(f32[64,256]{1,0:T(8,128)S(1)} %maximum_select_fusion.1), channel_id=1, source_target_pairs={{0,48},{16,32},{1,49},{17,33},{2,50},{18,34},{3,51},{19,35},{4,52}... | collective-permute-start | bytes 196616 | tf_op jit(solution)/shard_map/ppermute | solution.py:51
  31.1 1.3 %collective-permute-done.1 = f32[64,256]{1,0:T(8,128)S(1)} collective-permute-done((f32[64,256]{1,0:T(8,128)S(1)}, f32[64,256]{1,0:T(8,128)S(1)}, u32[]{:S(2)}, u32[]{:S(2)}) %collective-permute-start.1) | collective-permute-done | bytes 65568 | tf_op jit(solution)/shard_map/ppermute | solution.py:51
  32.5 10.9 %collective-permute-start.2 = (f32[64,256]{1,0:T(8,128)S(1)}, f32[64,256]{1,0:T(8,128)S(1)}, u32[]{:S(2)}, u32[]{:S(2)}) collective-permute-start(f32[64,256]{1,0:T(8,128)S(1)} %broadcast_select_fusion.3), channel_id=1, source_target_pairs={{0,8},{1,9},{16,24},{17,25},{32,40},{33,41},{48,56},{49,57},{64,72... | collective-permute-start | bytes 196616 | tf_op jit(solution)/shard_map/ppermute | solution.py:22
  43.3 1.3 %slice_bitcast_fusion.6 = (f32[128,256]{1,0:T(8,128)S(1)}, f32[128,256]{1,0:T(8,128)S(1)}, f32[128,256]{1,0:T(8,128)S(1)}, f32[128,256]{1,0:T(8,128)S(1)}, f32[1...) fusion(f32[8,128,256]{2,1,0:T(8,128)} %bitcast.48), kind=kLoop, calls=%fused_computation.15 | loop fusion | bytes 1835008 | tf_op jit(solution)/shard_map/squeeze | solution.py:34
  44.7 1.3 %collective-permute-start.6 = (f32[128,256]{1,0:T(8,128)S(1)}, f32[128,256]{1,0:T(8,128)S(1)}, u32[]{:S(2)}, u32[]{:S(2)}) collective-permute-start(f32[128,256]{1,0:T(8,128)S(1)} %get-tuple-element.11), channel_id=1, source_target_pairs={{0,2},{1,3},{16,18},{17,19},{32,34},{33,35},{48,50},{49,51},{64,66... | collective-permute-start | bytes 393224 | tf_op jit(solution)/shard_map/ppermute | solution.py:34
  46.0 1.3 %collective-permute-start.12 = (f32[128,256]{1,0:T(8,128)S(1)}, f32[128,256]{1,0:T(8,128)S(1)}, u32[]{:S(2)}, u32[]{:S(2)}) collective-permute-start(f32[128,256]{1,0:T(8,128)S(1)} %get-tuple-element.12), channel_id=1, source_target_pairs={{0,14},{1,15},{16,30},{17,31},{32,46},{33,47},{48,62},{49,63},{64,... | collective-permute-start | bytes 393224 | tf_op jit(solution)/shard_map/ppermute | solution.py:34
  47.3 1.3 %collective-permute-start.3 = (f32[64,256]{1,0:T(8,128)S(1)}, f32[64,256]{1,0:T(8,128)S(1)}, u32[]{:S(2)}, u32[]{:S(2)}) collective-permute-start(f32[64,256]{1,0:T(8,128)S(1)} %broadcast_select_fusion), channel_id=1, source_target_pairs={{0,4},{8,12},{1,5},{9,13},{16,20},{24,28},{17,21},{25,29},{32,36},... | collective-permute-start | bytes 196616 | tf_op jit(solution)/shard_map/ppermute | solution.py:22
  48.6 1.3 %collective-permute-start.11 = (f32[128,256]{1,0:T(8,128)S(1)}, f32[128,256]{1,0:T(8,128)S(1)}, u32[]{:S(2)}, u32[]{:S(2)}) collective-permute-start(f32[128,256]{1,0:T(8,128)S(1)} %get-tuple-element.13), channel_id=1, source_target_pairs={{0,12},{1,13},{16,28},{17,29},{32,44},{33,45},{48,60},{49,61},{64,... | collective-permute-start | bytes 393224 | tf_op jit(solution)/shard_map/ppermute | solution.py:34
  49.9 1.3 %collective-permute-start.10 = (f32[128,256]{1,0:T(8,128)S(1)}, f32[128,256]{1,0:T(8,128)S(1)}, u32[]{:S(2)}, u32[]{:S(2)}) collective-permute-start(f32[128,256]{1,0:T(8,128)S(1)} %get-tuple-element.14), channel_id=1, source_target_pairs={{0,10},{1,11},{16,26},{17,27},{32,42},{33,43},{48,58},{49,59},{64,... | collective-permute-start | bytes 393224 | tf_op jit(solution)/shard_map/ppermute | solution.py:34
  51.3 3.7 %collective-permute-start.9 = (f32[128,256]{1,0:T(8,128)S(1)}, f32[128,256]{1,0:T(8,128)S(1)}, u32[]{:S(2)}, u32[]{:S(2)}) collective-permute-start(f32[128,256]{1,0:T(8,128)S(1)} %get-tuple-element.15), channel_id=1, source_target_pairs={{0,8},{1,9},{16,24},{17,25},{32,40},{33,41},{48,56},{49,57},{64,72... | collective-permute-start | bytes 393224 | tf_op jit(solution)/shard_map/ppermute | solution.py:34
  55.0 1.3 %collective-permute-start.8 = (f32[128,256]{1,0:T(8,128)S(1)}, f32[128,256]{1,0:T(8,128)S(1)}, u32[]{:S(2)}, u32[]{:S(2)}) collective-permute-start(f32[128,256]{1,0:T(8,128)S(1)} %get-tuple-element.16), channel_id=1, source_target_pairs={{0,6},{1,7},{16,22},{17,23},{32,38},{33,39},{48,54},{49,55},{64,70... | collective-permute-start | bytes 393224 | tf_op jit(solution)/shard_map/ppermute | solution.py:34
  56.3 1.3 %collective-permute-start.7 = (f32[128,256]{1,0:T(8,128)S(1)}, f32[128,256]{1,0:T(8,128)S(1)}, u32[]{:S(2)}, u32[]{:S(2)}) collective-permute-start(f32[128,256]{1,0:T(8,128)S(1)} %get-tuple-element.17), channel_id=1, source_target_pairs={{0,4},{1,5},{16,20},{17,21},{32,36},{33,37},{48,52},{49,53},{64,68... | collective-permute-start | bytes 393224 | tf_op jit(solution)/shard_map/ppermute | solution.py:34
  57.6 1.3 %collective-permute-start.4 = (f32[64,256]{1,0:T(8,128)S(1)}, f32[64,256]{1,0:T(8,128)S(1)}, u32[]{:S(2)}, u32[]{:S(2)}) collective-permute-start(f32[64,256]{1,0:T(8,128)S(1)} %broadcast_select_fusion.1), channel_id=1, source_target_pairs={{0,2},{4,6},{8,10},{12,14},{1,3},{5,7},{9,11},{13,15},{16,18},{20,... | collective-permute-start | bytes 196616 | tf_op jit(solution)/shard_map/ppermute | solution.py:22
  59.0 0.7 collective-permute-done.7
  59.7 0.7 fusion.11
  60.5 0.1 broadcast_in_dim.34
  60.6 24.1 %all_to_all.11 = f32[8,128,256]{2,1,0:T(8,128)S(1)} all-to-all(f32[8,128,256]{2,1,0:T(8,128)S(1)} %broadcast_in_dim.34), channel_id=1, replica_groups=mesh['y'=8,'x'=4,'z'=8,'core'=2] {'y'}, dimensions={0} | all-to-all | bytes 2097152 | tf_op jit(solution)/shard_map/all_to_all | solution.py:54
  84.7 0.1 fusion.14
  84.8 10.0 %collective-permute-start.5 = (f32[512,256]{1,0:T(8,128)S(1)}, f32[512,256]{1,0:T(8,128)S(1)}, u32[]{:S(2)}, u32[]{:S(2)}) collective-permute-start(f32[512,256]{1,0:T(8,128)S(1)} %bitcast.54), channel_id=1, source_target_pairs={{0,1},{1,0},{2,3},{3,2},{4,5},{5,4},{6,7},{7,6},{8,9},{9,8},{10,11... | collective-permute-start | bytes 1572872 | tf_op jit(solution)/shard_map/ppermute | solution.py:57
  94.9 1.5 %collective-permute-done.5 = f32[512,256]{1,0:T(8,128)S(1)} collective-permute-done((f32[512,256]{1,0:T(8,128)S(1)}, f32[512,256]{1,0:T(8,128)S(1)}, u32[]{:S(2)}, u32[]{:S(2)}) %collective-permute-start.5) | collective-permute-done | bytes 524320 | tf_op jit(solution)/shard_map/ppermute | solution.py:57
  96.4 0.2 maximum_select_fusion.lead_ref
  96.6 18.2 %shard_map.17 = (f32[512,512]{1,0:T(8,128)S(1)}, f32[512,512]{1,0:T(8,128)S(1)}) custom-call(f32[512,512]{1,0:T(8,128)S(1)} %maximum_select_fusion.lead_ref), custom_call_target="tpu_custom_call" | custom-call | flops 2684354560 | bytes 3145728 | tf_op jit(solution)/shard_map/pallas_call | solution.py:159
  114.9 1.0 convolution_select_fusion
  115.9 1.8 %fusion.15 = f32[512,256]{1,0:T(8,128)S(1)} fusion(f32[512,512]{1,0:T(8,128)S(1)} %get-tuple-element.8, f32[512,256]{1,0:T(8,128)S(1)} %convolution_select_fusion), kind=kOutput, calls=%fused_computation.36 | convolution fusion | flops 805306368 | bytes 2097152 | tf_op jit(solution)/shard_map/dot_general | solution.py:184
  117.7 0.0 all-gather.3.cloned.1.call-done
  117.7 1.7 %fusion.13 = (f32[8,1,128,256]{3,2,1,0:T(8,128)S(1)}, f32[8,1,128,256]{3,2,1,0:T(8,128)S(1)}) fusion(f32[8,2,128,256]{3,2,1,0:T(8,128)} %bitcast.56), kind=kLoop, calls=%fused_computation.34 | loop fusion | bytes 4194304 | tf_op jit(solution)/shard_map/slice | solution.py:38
  119.4 1.8 %fusion = f32[1024,256]{1,0:T(8,128)S(1)} fusion(f32[512,256]{1,0:T(8,128)S(1)} %fusion.15, f32[1024,256]{1,0:T(8,128)S(1)} %bitcast.52, f32[1024,256]{1,0:T(8,128)S(1)} %bitcast.51), kind=kOutput, calls=%fused_computation | convolution fusion | flops 1611137024 | bytes 3670016 | tf_op jit(solution)/shard_map/dot_general | solution.py:188
  121.2 1.2 subtract_select_fusion
  (24 shorter events, 0.2 us)
Async XLA Ops:
  6.5 53.1 %copy-start = (f32[4,256,256]{2,1,0:T(8,128)S(1)}, f32[4,256,256]{2,1,0:T(8,128)}, u32[]{:S(2)}) copy-start(f32[4,256,256]{2,1,0:T(8,128)} %param.1) | copy-start | bytes 3145732
  6.5 111.2 %all-gather.3.cloned.1.call-start = ((), (), s32[]{:S(2)}) async-start(), calls=%async_computation.2 | async-start | bytes 2228224 | tf_op jit(solution)/shard_map/all_gather | solution.py:35
  24.3 5.5 %collective-permute-start = (f32[32,256]{1,0:T(8,128)S(1)}, f32[32,256]{1,0:T(8,128)S(1)}, u32[]{:S(2)}, u32[]{:S(2)}) collective-permute-start(f32[32,256]{1,0:T(8,128)S(1)} %slice_bitcast_fusion.7), channel_id=1, source_target_pairs={{0,16},{16,0},{1,17},{17,1},{2,18},{18,2},{3,19},{19,3},{4,20},{20... | collective-permute-start | bytes 98312 | tf_op jit(solution)/shard_map/ppermute | solution.py:49
  29.8 2.6 %collective-permute-start.1 = (f32[64,256]{1,0:T(8,128)S(1)}, f32[64,256]{1,0:T(8,128)S(1)}, u32[]{:S(2)}, u32[]{:S(2)}) collective-permute-start(f32[64,256]{1,0:T(8,128)S(1)} %maximum_select_fusion.1), channel_id=1, source_target_pairs={{0,48},{16,32},{1,49},{17,33},{2,50},{18,34},{3,51},{19,35},{4,52}... | collective-permute-start | bytes 196616 | tf_op jit(solution)/shard_map/ppermute | solution.py:51
  32.5 14.8 %collective-permute-start.2 = (f32[64,256]{1,0:T(8,128)S(1)}, f32[64,256]{1,0:T(8,128)S(1)}, u32[]{:S(2)}, u32[]{:S(2)}) collective-permute-start(f32[64,256]{1,0:T(8,128)S(1)} %broadcast_select_fusion.3), channel_id=1, source_target_pairs={{0,8},{1,9},{16,24},{17,25},{32,40},{33,41},{48,56},{49,57},{64,72... | collective-permute-start | bytes 196616 | tf_op jit(solution)/shard_map/ppermute | solution.py:22
  44.7 6.6 %collective-permute-start.6 = (f32[128,256]{1,0:T(8,128)S(1)}, f32[128,256]{1,0:T(8,128)S(1)}, u32[]{:S(2)}, u32[]{:S(2)}) collective-permute-start(f32[128,256]{1,0:T(8,128)S(1)} %get-tuple-element.11), channel_id=1, source_target_pairs={{0,2},{1,3},{16,18},{17,19},{32,34},{33,35},{48,50},{49,51},{64,66... | collective-permute-start | bytes 393224 | tf_op jit(solution)/shard_map/ppermute | solution.py:34
  46.0 9.0 %collective-permute-start.12 = (f32[128,256]{1,0:T(8,128)S(1)}, f32[128,256]{1,0:T(8,128)S(1)}, u32[]{:S(2)}, u32[]{:S(2)}) collective-permute-start(f32[128,256]{1,0:T(8,128)S(1)} %get-tuple-element.12), channel_id=1, source_target_pairs={{0,14},{1,15},{16,30},{17,31},{32,46},{33,47},{48,62},{49,63},{64,... | collective-permute-start | bytes 393224 | tf_op jit(solution)/shard_map/ppermute | solution.py:34
  47.3 9.0 %collective-permute-start.3 = (f32[64,256]{1,0:T(8,128)S(1)}, f32[64,256]{1,0:T(8,128)S(1)}, u32[]{:S(2)}, u32[]{:S(2)}) collective-permute-start(f32[64,256]{1,0:T(8,128)S(1)} %broadcast_select_fusion), channel_id=1, source_target_pairs={{0,4},{8,12},{1,5},{9,13},{16,20},{24,28},{17,21},{25,29},{32,36},... | collective-permute-start | bytes 196616 | tf_op jit(solution)/shard_map/ppermute | solution.py:22
  48.6 9.0 %collective-permute-start.11 = (f32[128,256]{1,0:T(8,128)S(1)}, f32[128,256]{1,0:T(8,128)S(1)}, u32[]{:S(2)}, u32[]{:S(2)}) collective-permute-start(f32[128,256]{1,0:T(8,128)S(1)} %get-tuple-element.13), channel_id=1, source_target_pairs={{0,12},{1,13},{16,28},{17,29},{32,44},{33,45},{48,60},{49,61},{64,... | collective-permute-start | bytes 393224 | tf_op jit(solution)/shard_map/ppermute | solution.py:34
  49.9 9.0 %collective-permute-start.10 = (f32[128,256]{1,0:T(8,128)S(1)}, f32[128,256]{1,0:T(8,128)S(1)}, u32[]{:S(2)}, u32[]{:S(2)}) collective-permute-start(f32[128,256]{1,0:T(8,128)S(1)} %get-tuple-element.14), channel_id=1, source_target_pairs={{0,10},{1,11},{16,26},{17,27},{32,42},{33,43},{48,58},{49,59},{64,... | collective-permute-start | bytes 393224 | tf_op jit(solution)/shard_map/ppermute | solution.py:34
  51.3 7.7 %collective-permute-start.9 = (f32[128,256]{1,0:T(8,128)S(1)}, f32[128,256]{1,0:T(8,128)S(1)}, u32[]{:S(2)}, u32[]{:S(2)}) collective-permute-start(f32[128,256]{1,0:T(8,128)S(1)} %get-tuple-element.15), channel_id=1, source_target_pairs={{0,8},{1,9},{16,24},{17,25},{32,40},{33,41},{48,56},{49,57},{64,72... | collective-permute-start | bytes 393224 | tf_op jit(solution)/shard_map/ppermute | solution.py:34
  55.0 4.0 %collective-permute-start.8 = (f32[128,256]{1,0:T(8,128)S(1)}, f32[128,256]{1,0:T(8,128)S(1)}, u32[]{:S(2)}, u32[]{:S(2)}) collective-permute-start(f32[128,256]{1,0:T(8,128)S(1)} %get-tuple-element.16), channel_id=1, source_target_pairs={{0,6},{1,7},{16,22},{17,23},{32,38},{33,39},{48,54},{49,55},{64,70... | collective-permute-start | bytes 393224 | tf_op jit(solution)/shard_map/ppermute | solution.py:34
  56.3 3.4 %collective-permute-start.7 = (f32[128,256]{1,0:T(8,128)S(1)}, f32[128,256]{1,0:T(8,128)S(1)}, u32[]{:S(2)}, u32[]{:S(2)}) collective-permute-start(f32[128,256]{1,0:T(8,128)S(1)} %get-tuple-element.17), channel_id=1, source_target_pairs={{0,4},{1,5},{16,20},{17,21},{32,36},{33,37},{48,52},{49,53},{64,68... | collective-permute-start | bytes 393224 | tf_op jit(solution)/shard_map/ppermute | solution.py:34
  57.6 2.8 %collective-permute-start.4 = (f32[64,256]{1,0:T(8,128)S(1)}, f32[64,256]{1,0:T(8,128)S(1)}, u32[]{:S(2)}, u32[]{:S(2)}) collective-permute-start(f32[64,256]{1,0:T(8,128)S(1)} %broadcast_select_fusion.1), channel_id=1, source_target_pairs={{0,2},{4,6},{8,10},{12,14},{1,3},{5,7},{9,11},{13,15},{16,18},{20,... | collective-permute-start | bytes 196616 | tf_op jit(solution)/shard_map/ppermute | solution.py:22
  84.8 11.6 %collective-permute-start.5 = (f32[512,256]{1,0:T(8,128)S(1)}, f32[512,256]{1,0:T(8,128)S(1)}, u32[]{:S(2)}, u32[]{:S(2)}) collective-permute-start(f32[512,256]{1,0:T(8,128)S(1)} %bitcast.54), channel_id=1, source_target_pairs={{0,1},{1,0},{2,3},{3,2},{4,5},{5,4},{6,7},{7,6},{8,9},{9,8},{10,11... | collective-permute-start | bytes 1572872 | tf_op jit(solution)/shard_map/ppermute | solution.py:57
Sparse Core Ops, SparseCore 0:
  60.5 44.2 all-gather.2
where the time goes:
time: 130 us; the launch traced here: 129 us
  blocking collectives  40.9 us (31%)
  starting transfers between devices  40.4 us (31%)
  Pallas kernels  18.2 us (14%)
  between operations  13.8 us (11%)
  waiting for transfers between devices  4.81 us (4%)
  matrix products  4.61 us (4%)
  local copies, waits for them, and re-layouts  4.3 us (3%)
  other arithmetic  2.18 us (2%)
    all_to_all x1, blocking collectives, top_rows(): got = lax.all_to_all(jnp.broadcast_to(sent, (high, *sent.shape)), 'y', 0, 0)  24.1 us
    pallas_call x1, Pallas kernels, factor_of(): pl.pallas_call(factor_kernel, out_shape=(shape, shape), scratch_shapes=[p...  18.2 us
    all_to_all x1, blocking collectives, top_rows(): mine = lax.all_to_all(choi[0].reshape(high, part, tile), 'y', 0, 0)[0]  16.7 us
    ppermute x3, starting transfers between devices, doubling(): sent = lax.ppermute(block, axis, pairs)  13.5 us
    ppermute x7, starting transfers between devices, panels_of(): piece = piece + lax.ppermute(flat[z], 'z', [(0, z)])  11.5 us
    ppermute x1, starting transfers between devices, top_rows(): pair = lax.ppermute(half, 'core', [(0, 1), (1, 0)])  10 us
    ppermute x1, starting transfers between devices, top_rows(): other = lax.ppermute(mine, 'x', [(0, 1), (1, 0)])  4.19 us
  transfers between devices with their start and end apart: 14, of which 4 were waited for; matrix products, arithmetic and copies ran while one was open for 4% of the time, Pallas kernels for 14%

commit v1 on v0

v1 whole, which is shorter than its diff:
```python
import jax
import jax.numpy as jnp
from jax import lax
from jax.experimental import pallas as pl
from jax.experimental.pallas import tpu as pltpu
from jax.sharding import Mesh
from jax.sharding import PartitionSpec as P

PANELS = 2
HIGHEST = lax.Precision.HIGHEST
STEPS = 40
FAR_STEPS = 6
NEAR = 0.1
LAST = 5e-4
ROW = ("y", "x")
COL = ("z", "core")


together = lax.optimization_barrier


def doubled(block, axis, step):
    size = lax.axis_size(axis)
    pairs = [(i, i + step) for i in range(0, size, 2 * step)]
    sent = lax.ppermute(block, axis, pairs)
    return jnp.where(lax.axis_index(axis) % (2 * step) == step, sent, block)


def scattered(block, axis):
    size = lax.axis_size(axis)
    parts = jnp.split(block, size)
    mine = jnp.where(lax.axis_index(axis) == 0, parts[0], 0.0)
    for i in range(1, size):
        mine = mine + lax.ppermute(parts[i], axis, [(0, i)])
    return mine


def gathered(block, axis):
    copies = jnp.broadcast_to(block, (lax.axis_size(axis), *block.shape))
    return lax.all_to_all(copies, axis, 0, 0)


def from_two(mine):
    x = lax.axis_index("x")
    near = lax.ppermute(mine, "x", [(0, 1), (1, 0)])
    even = lax.ppermute(mine, "x", [(0, 2), (1, 3)])
    odd = lax.ppermute(mine, "x", [(0, 3), (1, 2)])
    first = jnp.where(x == 0, mine, jnp.where(x == 1, near, jnp.where(x == 2, even, odd)))
    second = jnp.where(x == 1, mine, jnp.where(x == 0, near, jnp.where(x == 3, even, odd)))
    return jnp.concatenate([first, second])


def spread(choi):
    slots, tile, _ = choi.shape
    high = lax.axis_size("y")
    core = lax.axis_index("core")
    top = lax.all_to_all(choi[0].reshape(high, tile // high, tile), "y", 0, 0)[0]
    panel = scattered(choi.reshape(slots * tile, tile), "z")
    top = from_two(top)
    panel, top = together((panel, top))
    panels = lax.all_gather(panel, COL)
    lead = doubled(doubled(doubled(top, "z", 4), "z", 2), "z", 1)
    parts = gathered(jnp.concatenate([top, lead]), "y")
    parts = parts.reshape(high, 2 * PANELS, tile // high, tile).transpose(1, 0, 2, 3)
    column, half = parts.reshape(2, PANELS * tile, tile)
    pair = lax.ppermute(half, "core", [(0, 1), (1, 0)])
    left, right = jnp.where(core == 0, half, pair), jnp.where(core == 0, pair, half)
    lead = jnp.concatenate([left, right], axis=1)
    return column, lead, panels


def product(left, right, contract=((1,), (0,)), precision=HIGHEST):
    return lax.dot_general(
        left, right, (contract, ((), ())), precision=precision,
        preferred_element_type=jnp.float32,
    )


def rough(left, right, contract=((1,), (0,))):
    low = jnp.bfloat16
    left_high, right_high = left.astype(low), right.astype(low)
    left_rest = (left - left_high.astype(jnp.float32)).astype(low)
    right_rest = (right - right_high.astype(jnp.float32)).astype(low)
    small = product(left_high, right_rest, contract, None)
    small = small + product(left_rest, right_high, contract, None)
    return small + product(left_high, right_high, contract, None)


def square(block):
    return jnp.sum(block * block)


def eliminate(lead_ref, inverse_ref, work_ref):
    order = lead_ref.shape[0]
    rows = lax.broadcasted_iota(jnp.int32, (order, order), 0)
    cols = lax.broadcasted_iota(jnp.int32, (order, order), 1)
    work_ref[...] = lead_ref[...]
    inverse_ref[...] = (rows == cols).astype(jnp.float32)

    def pivot(k, carry):
        work = work_ref[...]
        column = jnp.sum(jnp.where(cols == k, work, 0.0), axis=1, keepdims=True)
        place = lax.broadcasted_iota(jnp.int32, (order, 1), 0)
        corner = jnp.sum(jnp.where(place == k, column, 0.0))
        scale = jnp.full((order, 1), corner)
        ratio = jnp.where(place > k, column / scale, 0.0)
        work_ref[...] = work - ratio * work_ref[pl.ds(k, 1), :]
        inverse = inverse_ref[...] - ratio * inverse_ref[pl.ds(k, 1), :]
        inverse_ref[...] = jnp.where(place == k, inverse / jnp.sqrt(scale), inverse)
        return carry

    lax.fori_loop(0, order, pivot, 0)


def weight_kernel(place_ref, lead_ref, column_ref, weight_ref, corner_ref, inverse_ref, work_ref):
    order = lead_ref.shape[0]
    half = order // 2
    rows = lax.broadcasted_iota(jnp.int32, (order, order), 0)
    cols = lax.broadcasted_iota(jnp.int32, (order, order), 1)
    same = rows == cols
    lead = lead_ref[...]
    down = lax.rsqrt(jnp.sum(jnp.where(same, lead, 0.0), axis=1, keepdims=True))
    along = lax.rsqrt(jnp.sum(jnp.where(same, lead, 0.0), axis=0, keepdims=True))
    scaled = lead * down * along
    off = jnp.where(same, 0.0, scaled).astype(jnp.bfloat16)
    twice = product(off, off, precision=None)
    bound = jnp.sqrt(jnp.sqrt(jnp.full((1, 1), square(twice))))
    shrink = jnp.where(bound < 1.0, jnp.ones_like(bound), 1.0 / (1.0 + bound))
    first = jnp.where(rows > cols, -scaled * shrink, jnp.where(same, 1.5 - 0.5 * shrink, 0.0))
    inverse_ref[...] = first * along * jnp.sqrt(shrink)

    top, low = pl.ds(0, half), pl.ds(half, half)
    small_rows = rows[:half, :half]
    small_cols = cols[:half, :half]
    unit = (small_rows == small_cols).astype(jnp.float32)
    across = ((1,), (1,))

    def lower(block):
        return jnp.where(small_rows > small_cols, block, 0.5 * unit * block)

    def step(multiply):
        x00, x10, x11 = inverse_ref[top, top], inverse_ref[low, top], inverse_ref[low, low]
        s00, s10 = lead_ref[top, top], lead_ref[low, top]
        s01, s11 = lead_ref[top, low], lead_ref[low, low]
        y00 = multiply(x00, s00)
        y10 = multiply(x10, s00) + multiply(x11, s10)
        y11 = multiply(x10, s01) + multiply(x11, s11)
        e00 = multiply(y00, x00, across) - unit
        e10 = multiply(y10, x00, across)
        e11 = multiply(y10, x10, across) + multiply(y11, x11, across) - unit
        residual = jnp.sqrt(square(e00) + 2.0 * square(e10) + square(e11))
        f00, f11 = lower(e00), lower(e11)
        inverse_ref[top, top] = x00 - multiply(f00, x00)
        inverse_ref[low, top] = x10 - multiply(e10, x00) - multiply(f11, x10)
        inverse_ref[low, low] = x11 - multiply(f11, x11)
        return residual

    def far(carry):
        count, residual = carry
        return (count < FAR_STEPS) & (residual > NEAR)

    def unfinished(carry):
        count, residual = carry
        return (count < STEPS) & (residual > LAST)

    start = (jnp.int32(0), jnp.float32(1.0))
    count, _ = lax.while_loop(far, lambda carry: (carry[0] + 1, step(rough)), start)
    start = (count, jnp.float32(1.0))
    _, residual = lax.while_loop(
        unfinished, lambda carry: (carry[0] + 1, step(product)), start
    )

    @pl.when(jnp.logical_not(residual <= LAST))
    def _():
        eliminate(lead_ref, inverse_ref, work_ref)

    x00, x10, x11 = inverse_ref[top, top], inverse_ref[low, top], inverse_ref[low, low]
    row, col = place_ref[0], place_ref[1]
    down = ((0,), (0,))

    @pl.when(col >= PANELS)
    def _():
        r0, r1 = column_ref[top, :], column_ref[low, :]
        h0 = product(x00, r0)
        h1 = product(x10, r0) + product(x11, r1)
        weight_ref[top, :] = product(x00, h0, down) + product(x10, h1, down)
        weight_ref[low, :] = product(x11, h1, down)
        corner_ref[...] = jnp.zeros((half, half), jnp.float32)

    @pl.when(col == 0)
    def _():
        weight_ref[top, :] = -x00.T
        weight_ref[low, :] = jnp.zeros((half, half), jnp.float32)
        corner = product(lead_ref[pl.ds(pl.multiple_of(jnp.minimum(row, 1) * half, half), half), top], x00, across)
        corner_ref[...] = jnp.where((row > 0) | (small_rows >= small_cols), corner, 0.0)

    @pl.when(col == 1)
    def _():
        weight_ref[top, :] = -x10.T
        weight_ref[low, :] = -x11.T
        corner = product(lead_ref[low, top], x10, across) + product(lead_ref[low, low], x11, across)
        corner_ref[...] = jnp.where((row > 0) & (small_rows >= small_cols), corner, 0.0)


def update_kernel(place_ref, panels_ref, weight_ref, corner_ref, choi_ref, out_ref):
    tile = out_ref.shape[1]
    row, col = place_ref[0], place_ref[1]
    top = (pl.program_id(0) == 0) & (row < PANELS)

    @pl.when(top)
    def _():
        out_ref[0] = corner_ref[...]

    @pl.when(jnp.logical_not(top))
    def _():
        base = jnp.where(col < PANELS, 0.0, choi_ref[0])
        for k in range(PANELS):
            panel = panels_ref[:, k].reshape(tile, tile)
            base = base - product(panel, weight_ref[pl.ds(k * tile, tile), :])
        out_ref[0] = base


def body(choi):
    slots, tile, _ = choi.shape
    order = PANELS * tile
    place = jnp.stack([lax.axis_index(ROW), lax.axis_index(COL)]).astype(jnp.int32)
    column, lead, panels = spread(choi)
    scalars = pl.BlockSpec(memory_space=pltpu.SMEM)
    vector = pl.BlockSpec(memory_space=pltpu.VMEM)
    weight, corner = pl.pallas_call(
        weight_kernel,
        in_specs=[scalars, vector, vector],
        out_shape=(
            jax.ShapeDtypeStruct((order, tile), jnp.float32),
            jax.ShapeDtypeStruct((tile, tile), jnp.float32),
        ),
        scratch_shapes=[pltpu.VMEM((order, order), jnp.float32)] * 2,
        compiler_params=pltpu.CompilerParams(vmem_limit_bytes=24 * 2**20),
        cost_estimate=pl.CostEstimate(
            flops=20 * order**3, bytes_accessed=12 * order * order, transcendentals=0
        ),
    )(place, lead, column)
    deep = panels.shape[0] // PANELS
    panels = panels.reshape(deep, PANELS, *panels.shape[1:])
    part = (deep // slots, *panels.shape[1:])
    one = pl.BlockSpec((1, tile, tile), lambda s: (s, 0, 0))
    return pl.pallas_call(
        update_kernel,
        grid=(slots,),
        in_specs=[
            scalars,
            pl.BlockSpec(part, lambda s: (s, 0, 0, 0)),
            pl.BlockSpec((order, tile), lambda s: (0, 0)),
            pl.BlockSpec((tile, tile), lambda s: (0, 0)),
            one,
        ],
        out_specs=one,
        out_shape=jax.ShapeDtypeStruct(choi.shape, jnp.float32),
        compiler_params=pltpu.CompilerParams(vmem_limit_bytes=16 * 2**20),
    )(place, panels, weight, corner, choi)


def solution(mesh):
    finer = Mesh(mesh.devices.reshape(8, 4, 8, 2), ("y", "x", "z", "core"))
    spec = P(None, ROW, COL)
    return jax.shard_map(
        body, mesh=finer, in_specs=(spec,), out_specs=spec, check_vma=False
    )
```

time: 130 us -> 119 us (0.915); the launches traced: 129 us -> 117 us
  blocking collectives: 40.9 us -> 29.2 us
  starting transfers between devices: 40.4 us -> 47.2 us
  matrix products: 4.61 us -> 0 us
  Pallas kernels: 18.2 us -> 15.1 us
    all_to_all x2 -> x1, blocking collectives: 40.9 us -> 29.2 us  [gathered(): return lax.all_to_all(copies, axis, 0, 0)]
    all_to_all x0 -> x1, starting transfers between devices: none -> 7.65 us  [spread(): lax.all_to_all(choi[0].reshape(high, tile // high, tile), 'y', 0, 0)[0]]
    dot_general x3 -> x0, matrix products: 4.61 us -> none  [the longest x1 1.81 us: body(): change = jnp.dot(panels, weight, precision=HIGHEST).reshape(choi.shape)]
    pallas_call x1 -> x2, Pallas kernels: 18.2 us -> 15.1 us  [the longest x1 11.8 us: body(): pl.pallas_call(weight_kernel, in_specs=[scalars, vector, vector], out_sha...]
    unnamed x2 -> x4, local copies, waits for them, and re-layouts: 0.01 us -> 1.59 us
    select_n x8 -> x5, other arithmetic: 1.43 us -> 0.11 us  [the longest x1 0.08 us: spread(): jnp.where(core == 0, half, pair)]
    split x0 -> x1, local copies, waits for them, and re-layouts: none -> 1.32 us  [scattered(): parts = jnp.split(block, size)]
    squeeze x2 -> x1, local copies, waits for them, and re-layouts: 1.32 us -> 0.01 us  [spread(): lax.all_to_all(choi[0].reshape(high, tile // high, tile), 'y', 0, 0)[0]]
  transfers between devices with their start and end apart: 14 -> 16, of which waited for: 4 -> 5; matrix products, arithmetic and copies ran while one was open for 4% -> 2% of each run, Pallas kernels for 14% -> 10%
where the time goes in v1:
time: 119 us; the launch traced here: 117 us
  starting transfers between devices  47.2 us (40%)
  blocking collectives  29.2 us (25%)
  Pallas kernels  15.1 us (13%)
  between operations  13.8 us (12%)
  waiting for transfers between devices  5.56 us (5%)
  local copies, waits for them, and re-layouts  4.89 us (4%)
    all_to_all x1, blocking collectives, gathered(): return lax.all_to_all(copies, axis, 0, 0)  29.2 us
    ppermute x7, starting transfers between devices, scattered(): mine = mine + lax.ppermute(parts[i], axis, [(0, i)])  16.5 us
    pallas_call x1, Pallas kernels, body(): pl.pallas_call(weight_kernel, in_specs=[scalars, vector, vector], out_sha...  11.8 us
    ppermute x1, starting transfers between devices, spread(): pair = lax.ppermute(half, 'core', [(0, 1), (1, 0)])  8.84 us
    all_to_all x1, starting transfers between devices, spread(): lax.all_to_all(choi[0].reshape(high, tile // high, tile), 'y', 0, 0)[0]  7.65 us
    ppermute x3, starting transfers between devices, doubled(): sent = lax.ppermute(block, axis, pairs)  7.51 us
    ppermute x3, waiting for transfers between devices, doubled(): sent = lax.ppermute(block, axis, pairs)  3.87 us
    pallas_call x1, Pallas kernels, body(): pl.pallas_call(update_kernel, grid=(slots,), in_specs=[scalars, pl.BlockS...  3.33 us
  transfers between devices with their start and end apart: 16, of which 5 were waited for; matrix products, arithmetic and copies ran while one was open for 2% of the time, Pallas kernels for 10%

profile of v1, /device:TPU:1, one launch (start us, length us, event | category | flops | bytes accessed | tf_op | source)
XLA Modules:
  0.0 116.8 jit_solution(10440269866630394449)
XLA Ops:
  6.5 1.8 %slice.8 = f32[1,256,256]{2,1,0:T(8,128)} slice(f32[4,256,256]{2,1,0:T(8,128)} %choi_ref.1), slice={[0:1], [0:256], [0:256]} | slice | bytes 524288 | tf_op jit(solution)/shard_map/slice | solution.py:57
  8.3 7.7 %all-to-all-start = ((f32[8,32,256]{2,1,0:T(8,128)}), f32[8,32,256]{2,1,0:T(8,128)S(1)}, u32[]{:S(2)}, u32[]{:S(2)}) async-start(f32[8,32,256]{2,1,0:T(8,128)} %bitcast.3), calls=%async_computation | async-start | bytes 524288 | tf_op jit(solution)/shard_map/all_to_all | solution.py:57
  16.0 1.3 %fusion.8 = (f32[128,256]{1,0:T(8,128)S(1)}, f32[128,256]{1,0:T(8,128)S(1)}, f32[128,256]{1,0:T(8,128)S(1)}, f32[128,256]{1,0:T(8,128)S(1)}, f32[128,256]{1,0:T(...) fusion(f32[1024,256]{1,0:T(8,128)} %bitcast.18), kind=kLoop, calls=%fused_computation.21 | loop fusion | bytes 1835008 | tf_op jit(solution)/shard_map/split | solution.py:31
  17.3 4.0 %collective-permute-start = (f32[128,256]{1,0:T(8,128)S(1)}, f32[128,256]{1,0:T(8,128)S(1)}, u32[]{:S(2)}, u32[]{:S(2)}) collective-permute-start(f32[128,256]{1,0:T(8,128)S(1)} %get-tuple-element.17), channel_id=1, source_target_pairs={{0,2},{1,3},{16,18},{17,19},{32,34},{33,35},{48,50},{49,51},{64,66... | collective-permute-start | bytes 393224 | tf_op jit(solution)/shard_map/ppermute | solution.py:34
  21.3 2.5 %collective-permute-start.1 = (f32[128,256]{1,0:T(8,128)S(1)}, f32[128,256]{1,0:T(8,128)S(1)}, u32[]{:S(2)}, u32[]{:S(2)}) collective-permute-start(f32[128,256]{1,0:T(8,128)S(1)} %get-tuple-element.23), channel_id=1, source_target_pairs={{0,4},{1,5},{16,20},{17,21},{32,36},{33,37},{48,52},{49,53},{64,68... | collective-permute-start | bytes 393224 | tf_op jit(solution)/shard_map/ppermute | solution.py:34
  23.8 2.5 %collective-permute-start.2 = (f32[128,256]{1,0:T(8,128)S(1)}, f32[128,256]{1,0:T(8,128)S(1)}, u32[]{:S(2)}, u32[]{:S(2)}) collective-permute-start(f32[128,256]{1,0:T(8,128)S(1)} %get-tuple-element.22), channel_id=1, source_target_pairs={{0,6},{1,7},{16,22},{17,23},{32,38},{33,39},{48,54},{49,55},{64,70... | collective-permute-start | bytes 393224 | tf_op jit(solution)/shard_map/ppermute | solution.py:34
  26.3 3.7 %collective-permute-start.3 = (f32[128,256]{1,0:T(8,128)S(1)}, f32[128,256]{1,0:T(8,128)S(1)}, u32[]{:S(2)}, u32[]{:S(2)}) collective-permute-start(f32[128,256]{1,0:T(8,128)S(1)} %get-tuple-element.21), channel_id=1, source_target_pairs={{0,8},{1,9},{16,24},{17,25},{32,40},{33,41},{48,56},{49,57},{64,72... | collective-permute-start | bytes 393224 | tf_op jit(solution)/shard_map/ppermute | solution.py:34
  30.0 1.3 %collective-permute-start.4 = (f32[128,256]{1,0:T(8,128)S(1)}, f32[128,256]{1,0:T(8,128)S(1)}, u32[]{:S(2)}, u32[]{:S(2)}) collective-permute-start(f32[128,256]{1,0:T(8,128)S(1)} %get-tuple-element.20), channel_id=1, source_target_pairs={{0,10},{1,11},{16,26},{17,27},{32,42},{33,43},{48,58},{49,59},{64,... | collective-permute-start | bytes 393224 | tf_op jit(solution)/shard_map/ppermute | solution.py:34
  31.3 1.3 %collective-permute-start.5 = (f32[128,256]{1,0:T(8,128)S(1)}, f32[128,256]{1,0:T(8,128)S(1)}, u32[]{:S(2)}, u32[]{:S(2)}) collective-permute-start(f32[128,256]{1,0:T(8,128)S(1)} %get-tuple-element.19), channel_id=1, source_target_pairs={{0,12},{1,13},{16,28},{17,29},{32,44},{33,45},{48,60},{49,61},{64,... | collective-permute-start | bytes 393224 | tf_op jit(solution)/shard_map/ppermute | solution.py:34
  32.6 1.3 %collective-permute-start.6 = (f32[128,256]{1,0:T(8,128)S(1)}, f32[128,256]{1,0:T(8,128)S(1)}, u32[]{:S(2)}, u32[]{:S(2)}) collective-permute-start(f32[128,256]{1,0:T(8,128)S(1)} %get-tuple-element.18), channel_id=1, source_target_pairs={{0,14},{1,15},{16,30},{17,31},{32,46},{33,47},{48,62},{49,63},{64,... | collective-permute-start | bytes 393224 | tf_op jit(solution)/shard_map/ppermute | solution.py:34
  34.0 3.1 %collective-permute-start.7 = (f32[32,256]{1,0:T(8,128)S(1)}, f32[32,256]{1,0:T(8,128)S(1)}, u32[]{:S(2)}, u32[]{:S(2)}) collective-permute-start(f32[32,256]{1,0:T(8,128)S(1)} %slice_bitcast_fusion), channel_id=1, source_target_pairs={{0,16},{16,0},{1,17},{17,1},{2,18},{18,2},{3,19},{19,3},{4,20},{20... | collective-permute-start | bytes 98312 | tf_op jit(solution)/shard_map/ppermute | solution.py:45
  37.1 2.2 %collective-permute-start.8 = (f32[32,256]{1,0:T(8,128)S(1)}, f32[32,256]{1,0:T(8,128)S(1)}, u32[]{:S(2)}, u32[]{:S(2)}) collective-permute-start(f32[32,256]{1,0:T(8,128)S(1)} %slice_bitcast_fusion), channel_id=1, source_target_pairs={{0,32},{16,48},{1,33},{17,49},{2,34},{18,50},{3,35},{19,51},{4,36}... | collective-permute-start | bytes 98312 | tf_op jit(solution)/shard_map/ppermute | solution.py:46
  39.3 1.3 %collective-permute-start.9 = (f32[32,256]{1,0:T(8,128)S(1)}, f32[32,256]{1,0:T(8,128)S(1)}, u32[]{:S(2)}, u32[]{:S(2)}) collective-permute-start(f32[32,256]{1,0:T(8,128)S(1)} %slice_bitcast_fusion), channel_id=1, source_target_pairs={{0,48},{16,32},{1,49},{17,33},{2,50},{18,34},{3,51},{19,35},{4,52}... | collective-permute-start | bytes 98312 | tf_op jit(solution)/shard_map/ppermute | solution.py:47
  40.7 0.7 fusion.6
  41.4 0.2 collective-permute-done.9
  41.7 4.9 %collective-permute-start.10 = (f32[64,256]{1,0:T(8,128)S(1)}, f32[64,256]{1,0:T(8,128)S(1)}, u32[]{:S(2)}, u32[]{:S(2)}) collective-permute-start(f32[64,256]{1,0:T(8,128)S(1)} %pad_maximum_fusion.2), channel_id=1, source_target_pairs={{0,8},{1,9},{16,24},{17,25},{32,40},{33,41},{48,56},{49,57},{64,72... | collective-permute-start | bytes 196616 | tf_op jit(solution)/shard_map/ppermute | solution.py:25
  46.6 1.3 %collective-permute-done.10 = f32[64,256]{1,0:T(8,128)S(1)} collective-permute-done((f32[64,256]{1,0:T(8,128)S(1)}, f32[64,256]{1,0:T(8,128)S(1)}, u32[]{:S(2)}, u32[]{:S(2)}) %collective-permute-start.10) | collective-permute-done | bytes 65568 | tf_op jit(solution)/shard_map/ppermute | solution.py:25
  47.9 1.3 %collective-permute-start.11 = (f32[64,256]{1,0:T(8,128)S(1)}, f32[64,256]{1,0:T(8,128)S(1)}, u32[]{:S(2)}, u32[]{:S(2)}) collective-permute-start(f32[64,256]{1,0:T(8,128)S(1)} %broadcast_select_fusion.2), channel_id=1, source_target_pairs={{0,4},{8,12},{1,5},{9,13},{16,20},{24,28},{17,21},{25,29},{32,36},... | collective-permute-start | bytes 196616 | tf_op jit(solution)/shard_map/ppermute | solution.py:25
  49.3 1.3 %collective-permute-done.11 = f32[64,256]{1,0:T(8,128)S(1)} collective-permute-done((f32[64,256]{1,0:T(8,128)S(1)}, f32[64,256]{1,0:T(8,128)S(1)}, u32[]{:S(2)}, u32[]{:S(2)}) %collective-permute-start.11) | collective-permute-done | bytes 65568 | tf_op jit(solution)/shard_map/ppermute | solution.py:25
  50.5 1.3 %collective-permute-start.12 = (f32[64,256]{1,0:T(8,128)S(1)}, f32[64,256]{1,0:T(8,128)S(1)}, u32[]{:S(2)}, u32[]{:S(2)}) collective-permute-start(f32[64,256]{1,0:T(8,128)S(1)} %broadcast_select_fusion.3), channel_id=1, source_target_pairs={{0,2},{4,6},{8,10},{12,14},{1,3},{5,7},{9,11},{13,15},{16,18},{20,... | collective-permute-start | bytes 196616 | tf_op jit(solution)/shard_map/ppermute | solution.py:25
  51.9 1.3 %collective-permute-done.12 = f32[64,256]{1,0:T(8,128)S(1)} collective-permute-done((f32[64,256]{1,0:T(8,128)S(1)}, f32[64,256]{1,0:T(8,128)S(1)}, u32[]{:S(2)}, u32[]{:S(2)}) %collective-permute-start.12) | collective-permute-done | bytes 65568 | tf_op jit(solution)/shard_map/ppermute | solution.py:25
  53.2 0.1 broadcast_in_dim.8
  53.3 29.2 %all_to_all.10 = f32[8,128,256]{2,1,0:T(8,128)S(1)} all-to-all(f32[8,128,256]{2,1,0:T(8,128)S(1)} %broadcast_in_dim.8), channel_id=1, replica_groups=mesh['y'=8,'x'=4,'z'=8,'core'=2] {'y'}, dimensions={0} | all-to-all | bytes 2097152 | tf_op jit(solution)/shard_map/all_to_all | solution.py:40
  82.5 0.1 fusion.7
  82.6 8.8 %collective-permute-start.13 = (f32[512,256]{1,0:T(8,128)S(1)}, f32[512,256]{1,0:T(8,128)S(1)}, u32[]{:S(2)}, u32[]{:S(2)}) collective-permute-start(f32[512,256]{1,0:T(8,128)S(1)} %bitcast.23), channel_id=1, source_target_pairs={{0,1},{1,0},{2,3},{3,2},{4,5},{5,4},{6,7},{7,6},{8,9},{9,8},{10,11... | collective-permute-start | bytes 1572872 | tf_op jit(solution)/shard_map/ppermute | solution.py:66
  91.5 0.1 pad_add_fusion.place_ref
  91.6 1.4 %collective-permute-done.13 = f32[512,256]{1,0:T(8,128)S(1)} collective-permute-done((f32[512,256]{1,0:T(8,128)S(1)}, f32[512,256]{1,0:T(8,128)S(1)}, u32[]{:S(2)}, u32[]{:S(2)}) %collective-permute-start.13) | collective-permute-done | bytes 524320 | tf_op jit(solution)/shard_map/ppermute | solution.py:66
  93.0 0.1 broadcast_select_fusion.1
  93.1 0.1 pad_maximum_fusion.lead_ref
  93.2 11.8 %shard_map.17 = (f32[512,256]{1,0:T(8,128)S(1)}, f32[256,256]{1,0:T(8,128)S(1)}) custom-call(s32[2]{0:T(128)S(1)} %pad_add_fusion.place_ref, f32[512,512]{1,0:T(8,128)S(1)} %pad_maximum_fusion.lead_ref, f32[512,256]{1,0:T(8,128)S(1)} %bitcast.21), custom_call_target="tpu_custom_call" | custom-call | flops 2684354560 | bytes 3145728 | tf_op jit(solution)/shard_map/pallas_call | solution.py:230
  105.0 1.6 %copy-done.1 = f32[2048,256]{1,0:T(8,128)S(1)} copy-done((f32[2048,256]{1,0:T(8,128)S(1)}, f32[2048,256]{1,0:T(8,128)}, u32[]{:S(2)}) %copy-start.1) | copy-done | bytes 2097176
  106.6 3.3 %shard_map.18 = f32[4,256,256]{2,1,0:T(8,128)} custom-call(s32[2]{0:T(128)S(1)} %pad_add_fusion.place_ref, f32[8,2,128,256]{3,2,1,0:T(8,128)S(1)} %bitcast.20, f32[512,256]{1,0:T(8,128)S(1)} %get-tuple-element.11.weight_ref, f32[256,256]{1,0:T(8,128)S(1)} %get-tuple-element.12.corner_ref, f32[4,256,256]{2,1,0:T(8,128)S(1)} %copy-done), custom_call_target="tpu_custom_call" | custom-call | tf_op jit(solution)/shard_map/pallas_call | solution.py:247
  (25 shorter events, 0.2 us)
Async XLA Ops:
  6.5 34.1 %copy-start = (f32[4,256,256]{2,1,0:T(8,128)S(1)}, f32[4,256,256]{2,1,0:T(8,128)}, u32[]{:S(2)}) copy-start(f32[4,256,256]{2,1,0:T(8,128)} %choi_ref.1) | copy-start | bytes 3145732
  8.3 25.7 %all-to-all-start = ((f32[8,32,256]{2,1,0:T(8,128)}), f32[8,32,256]{2,1,0:T(8,128)S(1)}, u32[]{:S(2)}, u32[]{:S(2)}) async-start(f32[8,32,256]{2,1,0:T(8,128)} %bitcast.3), calls=%async_computation | async-start | bytes 524288 | tf_op jit(solution)/shard_map/all_to_all | solution.py:57
  15.9 89.1 %all-gather.3.cloned.1.call-start = ((), (), s32[]{:S(2)}) async-start(), calls=%async_computation.2 | async-start | bytes 2228224 | tf_op jit(solution)/shard_map/all_gather | solution.py:61
  17.3 14.0 %collective-permute-start = (f32[128,256]{1,0:T(8,128)S(1)}, f32[128,256]{1,0:T(8,128)S(1)}, u32[]{:S(2)}, u32[]{:S(2)}) collective-permute-start(f32[128,256]{1,0:T(8,128)S(1)} %get-tuple-element.17), channel_id=1, source_target_pairs={{0,2},{1,3},{16,18},{17,19},{32,34},{33,35},{48,50},{49,51},{64,66... | collective-permute-start | bytes 393224 | tf_op jit(solution)/shard_map/ppermute | solution.py:34
  21.3 11.3 %collective-permute-start.1 = (f32[128,256]{1,0:T(8,128)S(1)}, f32[128,256]{1,0:T(8,128)S(1)}, u32[]{:S(2)}, u32[]{:S(2)}) collective-permute-start(f32[128,256]{1,0:T(8,128)S(1)} %get-tuple-element.23), channel_id=1, source_target_pairs={{0,4},{1,5},{16,20},{17,21},{32,36},{33,37},{48,52},{49,53},{64,68... | collective-permute-start | bytes 393224 | tf_op jit(solution)/shard_map/ppermute | solution.py:34
  23.8 10.2 %collective-permute-start.2 = (f32[128,256]{1,0:T(8,128)S(1)}, f32[128,256]{1,0:T(8,128)S(1)}, u32[]{:S(2)}, u32[]{:S(2)}) collective-permute-start(f32[128,256]{1,0:T(8,128)S(1)} %get-tuple-element.22), channel_id=1, source_target_pairs={{0,6},{1,7},{16,22},{17,23},{32,38},{33,39},{48,54},{49,55},{64,70... | collective-permute-start | bytes 393224 | tf_op jit(solution)/shard_map/ppermute | solution.py:34
  26.3 10.8 %collective-permute-start.3 = (f32[128,256]{1,0:T(8,128)S(1)}, f32[128,256]{1,0:T(8,128)S(1)}, u32[]{:S(2)}, u32[]{:S(2)}) collective-permute-start(f32[128,256]{1,0:T(8,128)S(1)} %get-tuple-element.21), channel_id=1, source_target_pairs={{0,8},{1,9},{16,24},{17,25},{32,40},{33,41},{48,56},{49,57},{64,72... | collective-permute-start | bytes 393224 | tf_op jit(solution)/shard_map/ppermute | solution.py:34
  30.0 9.3 %collective-permute-start.4 = (f32[128,256]{1,0:T(8,128)S(1)}, f32[128,256]{1,0:T(8,128)S(1)}, u32[]{:S(2)}, u32[]{:S(2)}) collective-permute-start(f32[128,256]{1,0:T(8,128)S(1)} %get-tuple-element.20), channel_id=1, source_target_pairs={{0,10},{1,11},{16,26},{17,27},{32,42},{33,43},{48,58},{49,59},{64,... | collective-permute-start | bytes 393224 | tf_op jit(solution)/shard_map/ppermute | solution.py:34
  31.3 9.3 %collective-permute-start.5 = (f32[128,256]{1,0:T(8,128)S(1)}, f32[128,256]{1,0:T(8,128)S(1)}, u32[]{:S(2)}, u32[]{:S(2)}) collective-permute-start(f32[128,256]{1,0:T(8,128)S(1)} %get-tuple-element.19), channel_id=1, source_target_pairs={{0,12},{1,13},{16,28},{17,29},{32,44},{33,45},{48,60},{49,61},{64,... | collective-permute-start | bytes 393224 | tf_op jit(solution)/shard_map/ppermute | solution.py:34
  32.6 8.0 %collective-permute-start.6 = (f32[128,256]{1,0:T(8,128)S(1)}, f32[128,256]{1,0:T(8,128)S(1)}, u32[]{:S(2)}, u32[]{:S(2)}) collective-permute-start(f32[128,256]{1,0:T(8,128)S(1)} %get-tuple-element.18), channel_id=1, source_target_pairs={{0,14},{1,15},{16,30},{17,31},{32,46},{33,47},{48,62},{49,63},{64,... | collective-permute-start | bytes 393224 | tf_op jit(solution)/shard_map/ppermute | solution.py:34
  34.0 7.4 %collective-permute-start.7 = (f32[32,256]{1,0:T(8,128)S(1)}, f32[32,256]{1,0:T(8,128)S(1)}, u32[]{:S(2)}, u32[]{:S(2)}) collective-permute-start(f32[32,256]{1,0:T(8,128)S(1)} %slice_bitcast_fusion), channel_id=1, source_target_pairs={{0,16},{16,0},{1,17},{17,1},{2,18},{18,2},{3,19},{19,3},{4,20},{20... | collective-permute-start | bytes 98312 | tf_op jit(solution)/shard_map/ppermute | solution.py:45
  37.1 4.3 %collective-permute-start.8 = (f32[32,256]{1,0:T(8,128)S(1)}, f32[32,256]{1,0:T(8,128)S(1)}, u32[]{:S(2)}, u32[]{:S(2)}) collective-permute-start(f32[32,256]{1,0:T(8,128)S(1)} %slice_bitcast_fusion), channel_id=1, source_target_pairs={{0,32},{16,48},{1,33},{17,49},{2,34},{18,50},{3,35},{19,51},{4,36}... | collective-permute-start | bytes 98312 | tf_op jit(solution)/shard_map/ppermute | solution.py:46
  39.3 2.3 %collective-permute-start.9 = (f32[32,256]{1,0:T(8,128)S(1)}, f32[32,256]{1,0:T(8,128)S(1)}, u32[]{:S(2)}, u32[]{:S(2)}) collective-permute-start(f32[32,256]{1,0:T(8,128)S(1)} %slice_bitcast_fusion), channel_id=1, source_target_pairs={{0,48},{16,32},{1,49},{17,33},{2,50},{18,34},{3,51},{19,35},{4,52}... | collective-permute-start | bytes 98312 | tf_op jit(solution)/shard_map/ppermute | solution.py:47
  41.7 6.2 %collective-permute-start.10 = (f32[64,256]{1,0:T(8,128)S(1)}, f32[64,256]{1,0:T(8,128)S(1)}, u32[]{:S(2)}, u32[]{:S(2)}) collective-permute-start(f32[64,256]{1,0:T(8,128)S(1)} %pad_maximum_fusion.2), channel_id=1, source_target_pairs={{0,8},{1,9},{16,24},{17,25},{32,40},{33,41},{48,56},{49,57},{64,72... | collective-permute-start | bytes 196616 | tf_op jit(solution)/shard_map/ppermute | solution.py:25
  47.9 2.6 %collective-permute-start.11 = (f32[64,256]{1,0:T(8,128)S(1)}, f32[64,256]{1,0:T(8,128)S(1)}, u32[]{:S(2)}, u32[]{:S(2)}) collective-permute-start(f32[64,256]{1,0:T(8,128)S(1)} %broadcast_select_fusion.2), channel_id=1, source_target_pairs={{0,4},{8,12},{1,5},{9,13},{16,20},{24,28},{17,21},{25,29},{32,36},... | collective-permute-start | bytes 196616 | tf_op jit(solution)/shard_map/ppermute | solution.py:25
  50.5 2.6 %collective-permute-start.12 = (f32[64,256]{1,0:T(8,128)S(1)}, f32[64,256]{1,0:T(8,128)S(1)}, u32[]{:S(2)}, u32[]{:S(2)}) collective-permute-start(f32[64,256]{1,0:T(8,128)S(1)} %broadcast_select_fusion.3), channel_id=1, source_target_pairs={{0,2},{4,6},{8,10},{12,14},{1,3},{5,7},{9,11},{13,15},{16,18},{20,... | collective-permute-start | bytes 196616 | tf_op jit(solution)/shard_map/ppermute | solution.py:25
  82.6 10.4 %collective-permute-start.13 = (f32[512,256]{1,0:T(8,128)S(1)}, f32[512,256]{1,0:T(8,128)S(1)}, u32[]{:S(2)}, u32[]{:S(2)}) collective-permute-start(f32[512,256]{1,0:T(8,128)S(1)} %bitcast.23), channel_id=1, source_target_pairs={{0,1},{1,0},{2,3},{3,2},{4,5},{5,4},{6,7},{7,6},{8,9},{9,8},{10,11... | collective-permute-start | bytes 1572872 | tf_op jit(solution)/shard_map/ppermute | solution.py:66
  105.0 1.6 %copy-start.1 = (f32[2048,256]{1,0:T(8,128)S(1)}, f32[2048,256]{1,0:T(8,128)}, u32[]{:S(2)}) copy-start(f32[2048,256]{1,0:T(8,128)} %all-gather.3.cloned.1.call-done) | copy-start | bytes 6291460
Sparse Core Ops, SparseCore 0:
  49.4 48.9 all-gather.2

commit v2 on v1

--- a/solution.py
+++ b/solution.py
@@ -28,11 +28,18 @@
 
 def scattered(block, axis):
     size = lax.axis_size(axis)
-    parts = jnp.split(block, size)
+    parts = jnp.split(block, size // 2)
     mine = jnp.where(lax.axis_index(axis) == 0, parts[0], 0.0)
-    for i in range(1, size):
-        mine = mine + lax.ppermute(parts[i], axis, [(0, i)])
+    for i in range(1, size // 2):
+        mine = mine + lax.ppermute(parts[i], axis, [(0, 2 * i)])
     return mine
+
+
+def halved(block, axis):
+    size = lax.axis_size(axis)
+    keep, give = jnp.split(block, 2)
+    sent = lax.ppermute(give, axis, [(i, i + 1) for i in range(0, size, 2)])
+    return jnp.where(lax.axis_index(axis) % 2 == 1, sent, keep)
 
 
 def gathered(block, axis):
@@ -50,6 +57,12 @@
     return jnp.concatenate([first, second])
 
 
+def stacked(parts, tile):
+    high, double, width = parts.shape
+    parts = parts.reshape(high, 2, double // 2, width).transpose(1, 0, 2, 3)
+    return parts.reshape(2 * tile, width)
+
+
 def spread(choi):
     slots, tile, _ = choi.shape
     high = lax.axis_size("y")
@@ -58,11 +71,15 @@
     panel = scattered(choi.reshape(slots * tile, tile), "z")
     top = from_two(top)
     panel, top = together((panel, top))
+    panel = halved(panel, "z")
+    lead = doubled(top, "z", 4)
+    panel, lead = together((panel, lead))
     panels = lax.all_gather(panel, COL)
-    lead = doubled(doubled(doubled(top, "z", 4), "z", 2), "z", 1)
-    parts = gathered(jnp.concatenate([top, lead]), "y")
-    parts = parts.reshape(high, 2 * PANELS, tile // high, tile).transpose(1, 0, 2, 3)
-    column, half = parts.reshape(2, PANELS * tile, tile)
+    column = gathered(top, "y")
+    lead = doubled(doubled(lead, "z", 2), "z", 1)
+    lead, column = together((lead, column))
+    lead = gathered(lead, "y")
+    column, half = stacked(column, tile), stacked(lead, tile)
     pair = lax.ppermute(half, "core", [(0, 1), (1, 0)])
     left, right = jnp.where(core == 0, half, pair), jnp.where(core == 0, pair, half)
     lead = jnp.concatenate([left, right], axis=1)
@@ -74,6 +91,10 @@
         left, right, (contract, ((), ())), precision=precision,
         preferred_element_type=jnp.float32,
     )
+
+
+def coarse(left, right, contract=((1,), (0,))):
+    return product(left.astype(jnp.bfloat16), right.astype(jnp.bfloat16), contract, None)
 
 
 def rough(left, right, contract=((1,), (0,))):
@@ -112,7 +133,9 @@
     lax.fori_loop(0, order, pivot, 0)
 
 
-def weight_kernel(place_ref, lead_ref, column_ref, weight_ref, corner_ref, inverse_ref, work_ref):
+def update_kernel(
+    place_ref, lead_ref, column_ref, panels_ref, choi_ref, out_ref, inverse_ref, work_ref, weight_ref, corner_ref
+):
     order = lead_ref.shape[0]
     half = order // 2
     rows = lax.broadcasted_iota(jnp.int32, (order, order), 0)
@@ -163,7 +186,7 @@
         count, residual = carry
         return (count < STEPS) & (residual > LAST)
 
-    start = (jnp.int32(0), jnp.float32(1.0))
+    start = (jnp.int32(1), step(coarse))
     count, _ = lax.while_loop(far, lambda carry: (carry[0] + 1, step(rough)), start)
     start = (count, jnp.float32(1.0))
     _, residual = lax.while_loop(
@@ -201,23 +224,16 @@
         corner = product(lead_ref[low, top], x10, across) + product(lead_ref[low, low], x11, across)
         corner_ref[...] = jnp.where((row > 0) & (small_rows >= small_cols), corner, 0.0)
 
-
-def update_kernel(place_ref, panels_ref, weight_ref, corner_ref, choi_ref, out_ref):
-    tile = out_ref.shape[1]
-    row, col = place_ref[0], place_ref[1]
-    top = (pl.program_id(0) == 0) & (row < PANELS)
-
-    @pl.when(top)
+    for slot in range(choi_ref.shape[0]):
+        base = jnp.where(col < PANELS, 0.0, choi_ref[slot])
+        for k in range(PANELS):
+            panel = panels_ref[slot, :, k].reshape(half, half)
+            base = base - product(panel, weight_ref[pl.ds(k * half, half), :])
+        out_ref[slot] = base
+
+    @pl.when(row < PANELS)
     def _():
         out_ref[0] = corner_ref[...]
-
-    @pl.when(jnp.logical_not(top))
-    def _():
-        base = jnp.where(col < PANELS, 0.0, choi_ref[0])
-        for k in range(PANELS):
-            panel = panels_ref[:, k].reshape(tile, tile)
-            base = base - product(panel, weight_ref[pl.ds(k * tile, tile), :])
-        out_ref[0] = base
 
 
 def body(choi):
@@ -225,39 +241,22 @@
     order = PANELS * tile
     place = jnp.stack([lax.axis_index(ROW), lax.axis_index(COL)]).astype(jnp.int32)
     column, lead, panels = spread(choi)
-    scalars = pl.BlockSpec(memory_space=pltpu.SMEM)
+    deep = panels.shape[0] // PANELS
+    panels = panels.reshape(slots, deep // slots, PANELS, *panels.shape[1:])
     vector = pl.BlockSpec(memory_space=pltpu.VMEM)
-    weight, corner = pl.pallas_call(
-        weight_kernel,
-        in_specs=[scalars, vector, vector],
-        out_shape=(
-            jax.ShapeDtypeStruct((order, tile), jnp.float32),
-            jax.ShapeDtypeStruct((tile, tile), jnp.float32),
-        ),
-        scratch_shapes=[pltpu.VMEM((order, order), jnp.float32)] * 2,
-        compiler_params=pltpu.CompilerParams(vmem_limit_bytes=24 * 2**20),
-        cost_estimate=pl.CostEstimate(
-            flops=20 * order**3, bytes_accessed=12 * order * order, transcendentals=0
-        ),
-    )(place, lead, column)
-    deep = panels.shape[0] // PANELS
-    panels = panels.reshape(deep, PANELS, *panels.shape[1:])
-    part = (deep // slots, *panels.shape[1:])
-    one = pl.BlockSpec((1, tile, tile), lambda s: (s, 0, 0))
     return pl.pallas_call(
         update_kernel,
-        grid=(slots,),
-        in_specs=[
-            scalars,
-            pl.BlockSpec(part, lambda s: (s, 0, 0, 0)),
-            pl.BlockSpec((order, tile), lambda s: (0, 0)),
-            pl.BlockSpec((tile, tile), lambda s: (0, 0)),
-            one,
+        in_specs=[pl.BlockSpec(memory_space=pltpu.SMEM)] + [vector] * 4,
+        out_specs=vector,
+        out_shape=jax.ShapeDtypeStruct(choi.shape, jnp.float32),
+        scratch_shapes=[
+            pltpu.VMEM((order, order), jnp.float32),
+            pltpu.VMEM((order, order), jnp.float32),
+            pltpu.VMEM((order, tile), jnp.float32),
+            pltpu.VMEM((tile, tile), jnp.float32),
         ],
-        out_specs=one,
-        out_shape=jax.ShapeDtypeStruct(choi.shape, jnp.float32),
-        compiler_params=pltpu.CompilerParams(vmem_limit_bytes=16 * 2**20),
-    )(place, panels, weight, corner, choi)
+        compiler_params=pltpu.CompilerParams(vmem_limit_bytes=32 * 2**20),
+    )(place, lead, column, panels, choi)
 
 
 def solution(mesh):

time: 119 us -> 115 us (0.966)
  blocking collectives: 29.2 us -> 15 us
  waiting for transfers between devices: 5.56 us -> 14.1 us
  starting transfers between devices: 47.2 us -> 51.4 us
  Pallas kernels: 15.1 us -> 13.8 us
    all_to_all x1, blocking collectives: 29.2 us -> 15 us  [gathered(): return lax.all_to_all(copies, axis, 0, 0)]
    all_to_all x0 -> x1, waiting for transfers between devices: none -> 6.91 us  [gathered(): return lax.all_to_all(copies, axis, 0, 0)]
    ppermute x3, starting transfers between devices: 7.51 us -> 11.4 us  [doubled(): sent = lax.ppermute(block, axis, pairs)]
    all_to_all x0 -> x1, starting transfers between devices: none -> 3.49 us  [gathered(): return lax.all_to_all(copies, axis, 0, 0)]
    ppermute x7 -> x4, starting transfers between devices: 16.5 us -> 13.9 us  [the longest x3 12.6 us: scattered(): mine = mine + lax.ppermute(parts[i], axis, [(0, 2 * i)])]
    ppermute x7 -> x4, waiting for transfers between devices: 0.02 us -> 1.9 us  [the longest x1 1.89 us: halved(): sent = lax.ppermute(give, axis, [(i, i + 1) for i in range(0, size, 2)])]
    slice x1 -> x0, local copies, waits for them, and re-layouts: 1.76 us -> none  [spread(): choi[0].reshape(high, tile // high, tile)]
    pallas_call x2 -> x1, Pallas kernels: 15.1 us -> 13.8 us  [body(): pl.pallas_call(update_kernel, in_specs=[pl.BlockSpec(memory_space=pltpu.S...]
  transfers between devices with their start and end apart: 16 -> 14, of which waited for: 5 -> 7; matrix products, arithmetic and copies ran while one was open for 2% -> 1% of each run, Pallas kernels for 10% -> 0%
where the time goes in v2:
time: 115 us; the launch traced here: 114 us
  starting transfers between devices  51.4 us (45%)
  blocking collectives  15 us (13%)
  waiting for transfers between devices  14.1 us (12%)
  Pallas kernels  13.8 us (12%)
  between operations  13.7 us (12%)
  local copies, waits for them, and re-layouts  4.64 us (4%)
    all_to_all x1, blocking collectives, gathered(): return lax.all_to_all(copies, axis, 0, 0)  15 us
    pallas_call x1, Pallas kernels, body(): pl.pallas_call(update_kernel, in_specs=[pl.BlockSpec(memory_space=pltpu.S...  13.8 us
    ppermute x3, starting transfers between devices, scattered(): mine = mine + lax.ppermute(parts[i], axis, [(0, 2 * i)])  12.6 us
    ppermute x3, starting transfers between devices, doubled(): sent = lax.ppermute(block, axis, pairs)  11.4 us
    ppermute x1, starting transfers between devices, spread(): pair = lax.ppermute(half, 'core', [(0, 1), (1, 0)])  8.3 us
    all_to_all x1, starting transfers between devices, spread(): lax.all_to_all(choi[0].reshape(high, tile // high, tile), 'y', 0, 0)[0]  7.65 us
    all_to_all x1, waiting for transfers between devices, gathered(): return lax.all_to_all(copies, axis, 0, 0)  6.91 us
    all_to_all x1, starting transfers between devices, gathered(): return lax.all_to_all(copies, axis, 0, 0)  3.49 us
  transfers between devices with their start and end apart: 14, of which 7 were waited for; matrix products, arithmetic and copies ran while one was open for 1% of the time, Pallas kernels for 0%

profile of v2, /device:TPU:1, one launch (start us, length us, event | category | flops | bytes accessed | tf_op | source)
XLA Modules:
  0.0 113.8 jit_solution(11436359159998826298)
XLA Ops:
  6.5 2.1 %fusion.2 = (f32[1,256,256]{2,1,0:T(8,128)}, f32[256,256]{1,0:T(8,128)S(1)}, f32[256,256]{1,0:T(8,128)S(1)}, f32[256,256]{1,0:T(8,128)S(1)}) fusion(f32[4,256,256]{2,1,0:T(8,128)} %choi_ref.1), kind=kLoop, calls=%fused_computation.18 | loop fusion | bytes 2097152 | tf_op jit(solution)/shard_map/split | solution.py:31
  8.6 7.7 %all-to-all-start = ((f32[8,32,256]{2,1,0:T(8,128)}), f32[8,32,256]{2,1,0:T(8,128)S(1)}, u32[]{:S(2)}, u32[]{:S(2)}) async-start(f32[8,32,256]{2,1,0:T(8,128)} %bitcast.6), calls=%async_computation | async-start | bytes 524288 | tf_op jit(solution)/shard_map/all_to_all | solution.py:70
  16.3 0.0 all-gather.3.cloned.1.call-start
  16.3 5.8 %collective-permute-start = (f32[256,256]{1,0:T(8,128)S(1)}, f32[256,256]{1,0:T(8,128)S(1)}, u32[]{:S(2)}, u32[]{:S(2)}) collective-permute-start(f32[256,256]{1,0:T(8,128)S(1)} %get-tuple-element.21), channel_id=1, source_target_pairs={{0,4},{1,5},{16,20},{17,21},{32,36},{33,37},{48,52},{49,53},{64,68... | collective-permute-start | bytes 786440 | tf_op jit(solution)/shard_map/ppermute | solution.py:34
  22.1 5.5 %collective-permute-start.1 = (f32[256,256]{1,0:T(8,128)S(1)}, f32[256,256]{1,0:T(8,128)S(1)}, u32[]{:S(2)}, u32[]{:S(2)}) collective-permute-start(f32[256,256]{1,0:T(8,128)S(1)} %get-tuple-element.20), channel_id=1, source_target_pairs={{0,8},{1,9},{16,24},{17,25},{32,40},{33,41},{48,56},{49,57},{64,72... | collective-permute-start | bytes 786440 | tf_op jit(solution)/shard_map/ppermute | solution.py:34
  27.7 1.3 %collective-permute-start.2 = (f32[256,256]{1,0:T(8,128)S(1)}, f32[256,256]{1,0:T(8,128)S(1)}, u32[]{:S(2)}, u32[]{:S(2)}) collective-permute-start(f32[256,256]{1,0:T(8,128)S(1)} %get-tuple-element.22), channel_id=1, source_target_pairs={{0,12},{1,13},{16,28},{17,29},{32,44},{33,45},{48,60},{49,61},{64,... | collective-permute-start | bytes 786440 | tf_op jit(solution)/shard_map/ppermute | solution.py:34
  29.0 3.1 %collective-permute-start.3 = (f32[32,256]{1,0:T(8,128)S(1)}, f32[32,256]{1,0:T(8,128)S(1)}, u32[]{:S(2)}, u32[]{:S(2)}) collective-permute-start(f32[32,256]{1,0:T(8,128)S(1)} %slice_bitcast_fusion.3), channel_id=1, source_target_pairs={{0,16},{16,0},{1,17},{17,1},{2,18},{18,2},{3,19},{19,3},{4,20},{20... | collective-permute-start | bytes 98312 | tf_op jit(solution)/shard_map/ppermute | solution.py:52
  32.1 2.2 %collective-permute-start.4 = (f32[32,256]{1,0:T(8,128)S(1)}, f32[32,256]{1,0:T(8,128)S(1)}, u32[]{:S(2)}, u32[]{:S(2)}) collective-permute-start(f32[32,256]{1,0:T(8,128)S(1)} %slice_bitcast_fusion.3), channel_id=1, source_target_pairs={{0,32},{16,48},{1,33},{17,49},{2,34},{18,50},{3,35},{19,51},{4,36}... | collective-permute-start | bytes 98312 | tf_op jit(solution)/shard_map/ppermute | solution.py:53
  34.4 1.3 %collective-permute-start.5 = (f32[32,256]{1,0:T(8,128)S(1)}, f32[32,256]{1,0:T(8,128)S(1)}, u32[]{:S(2)}, u32[]{:S(2)}) collective-permute-start(f32[32,256]{1,0:T(8,128)S(1)} %slice_bitcast_fusion.3), channel_id=1, source_target_pairs={{0,48},{16,32},{1,49},{17,33},{2,50},{18,34},{3,51},{19,35},{4,52}... | collective-permute-start | bytes 98312 | tf_op jit(solution)/shard_map/ppermute | solution.py:54
  35.7 0.1 fusion.1
  35.8 0.9 collective-permute-done.5
  36.7 8.3 %collective-permute-start.7 = (f32[64,256]{1,0:T(8,128)S(1)}, f32[64,256]{1,0:T(8,128)S(1)}, u32[]{:S(2)}, u32[]{:S(2)}) collective-permute-start(f32[64,256]{1,0:T(8,128)S(1)} %pad_maximum_fusion.1), channel_id=1, source_target_pairs={{0,8},{1,9},{16,24},{17,25},{32,40},{33,41},{48,56},{49,57},{64,72... | collective-permute-start | bytes 196616 | tf_op jit(solution)/shard_map/ppermute | solution.py:25
  45.0 1.3 %collective-permute-start.6 = (f32[128,256]{1,0:T(8,128)S(1)}, f32[128,256]{1,0:T(8,128)S(1)}, u32[]{:S(2)}, u32[]{:S(2)}) collective-permute-start(f32[128,256]{1,0:T(8,128)S(1)} %split.31), channel_id=1, source_target_pairs={{0,2},{4,6},{8,10},{12,14},{1,3},{5,7},{9,11},{13,15},{16,18},{20,... | collective-permute-start | bytes 393224 | tf_op jit(solution)/shard_map/ppermute | solution.py:41
  46.3 1.9 %collective-permute-done.6 = f32[128,256]{1,0:T(8,128)S(1)} collective-permute-done((f32[128,256]{1,0:T(8,128)S(1)}, f32[128,256]{1,0:T(8,128)S(1)}, u32[]{:S(2)}, u32[]{:S(2)}) %collective-permute-start.6) | collective-permute-done | bytes 131104 | tf_op jit(solution)/shard_map/ppermute | solution.py:41
  48.2 0.7 slice_select_fusion
  48.9 0.0 all-gather.3.cloned.1.call-update
  48.9 0.8 broadcast_in_dim.11
  49.8 3.5 %all-to-all-start.1 = ((f32[8,64,256]{2,1,0:T(8,128)}), f32[8,64,256]{2,1,0:T(8,128)S(1)}, u32[]{:S(2)}, u32[]{:S(2)}) async-start(f32[8,64,256]{2,1,0:T(8,128)} %broadcast_in_dim.11), calls=%async_computation.1 | async-start | bytes 1048576 | tf_op jit(solution)/shard_map/all_to_all | solution.py:47
  53.3 1.3 %collective-permute-start.8 = (f32[64,256]{1,0:T(8,128)S(1)}, f32[64,256]{1,0:T(8,128)S(1)}, u32[]{:S(2)}, u32[]{:S(2)}) collective-permute-start(f32[64,256]{1,0:T(8,128)S(1)} %broadcast_select_fusion.2), channel_id=1, source_target_pairs={{0,4},{8,12},{1,5},{9,13},{16,20},{24,28},{17,21},{25,29},{32,36},... | collective-permute-start | bytes 196616 | tf_op jit(solution)/shard_map/ppermute | solution.py:25
  54.6 1.3 %collective-permute-done.8 = f32[64,256]{1,0:T(8,128)S(1)} collective-permute-done((f32[64,256]{1,0:T(8,128)S(1)}, f32[64,256]{1,0:T(8,128)S(1)}, u32[]{:S(2)}, u32[]{:S(2)}) %collective-permute-start.8) | collective-permute-done | bytes 65568 | tf_op jit(solution)/shard_map/ppermute | solution.py:25
  55.9 1.9 %collective-permute-start.9 = (f32[64,256]{1,0:T(8,128)S(1)}, f32[64,256]{1,0:T(8,128)S(1)}, u32[]{:S(2)}, u32[]{:S(2)}) collective-permute-start(f32[64,256]{1,0:T(8,128)S(1)} %broadcast_select_fusion.3), channel_id=1, source_target_pairs={{0,2},{4,6},{8,10},{12,14},{1,3},{5,7},{9,11},{13,15},{16,18},{20,... | collective-permute-start | bytes 196616 | tf_op jit(solution)/shard_map/ppermute | solution.py:25
  57.8 1.3 %collective-permute-done.9 = f32[64,256]{1,0:T(8,128)S(1)} collective-permute-done((f32[64,256]{1,0:T(8,128)S(1)}, f32[64,256]{1,0:T(8,128)S(1)}, u32[]{:S(2)}, u32[]{:S(2)}) %collective-permute-start.9) | collective-permute-done | bytes 65568 | tf_op jit(solution)/shard_map/ppermute | solution.py:25
  59.1 6.9 %all-to-all-done.1 = f32[8,64,256]{2,1,0:T(8,128)S(1)} async-done(((f32[8,64,256]{2,1,0:T(8,128)}), f32[8,64,256]{2,1,0:T(8,128)S(1)}, u32[]{:S(2)}, u32[]{:S(2)}) %all-to-all-start.1) | async-done | bytes 524320 | tf_op jit(solution)/shard_map/all_to_all | solution.py:47
  66.0 15.0 %all_to_all.15 = f32[8,64,256]{2,1,0:T(8,128)S(1)} all-to-all(f32[8,64,256]{2,1,0:T(8,128)S(1)} %broadcast_in_dim.12), channel_id=1, replica_groups=mesh['y'=8,'x'=4,'z'=8,'core'=2] {'y'}, dimensions={0} | all-to-all | bytes 1048576 | tf_op jit(solution)/shard_map/all_to_all | solution.py:47
  81.1 8.3 %collective-permute-start.10 = (f32[512,256]{1,0:T(8,128)S(1)}, f32[512,256]{1,0:T(8,128)S(1)}, u32[]{:S(2)}, u32[]{:S(2)}) collective-permute-start(f32[512,256]{1,0:T(8,128)S(1)} %bitcast.34), channel_id=1, source_target_pairs={{0,1},{1,0},{2,3},{3,2},{4,5},{5,4},{6,7},{7,6},{8,9},{9,8},{10,11... | collective-permute-start | bytes 1572872 | tf_op jit(solution)/shard_map/ppermute | solution.py:83
  89.4 0.1 pad_add_fusion.place_ref
  89.5 1.4 %collective-permute-done.10 = f32[512,256]{1,0:T(8,128)S(1)} collective-permute-done((f32[512,256]{1,0:T(8,128)S(1)}, f32[512,256]{1,0:T(8,128)S(1)}, u32[]{:S(2)}, u32[]{:S(2)}) %collective-permute-start.10) | collective-permute-done | bytes 524320 | tf_op jit(solution)/shard_map/ppermute | solution.py:83
  90.9 0.1 broadcast_select_fusion.1
  91.0 0.1 pad_maximum_fusion.lead_ref
  91.1 0.4 all-gather.3.cloned.1.call-done
  91.5 1.6 %copy-done.1 = f32[2048,256]{1,0:T(8,128)S(1)} copy-done((f32[2048,256]{1,0:T(8,128)S(1)}, f32[2048,256]{1,0:T(8,128)}, u32[]{:S(2)}) %copy-start.1) | copy-done | bytes 2097176
  93.1 13.8 %shard_map.17 = f32[4,256,256]{2,1,0:T(8,128)} custom-call(s32[2]{0:T(128)S(1)} %pad_add_fusion.place_ref, f32[512,512]{1,0:T(8,128)S(1)} %pad_maximum_fusion.lead_ref, f32[512,256]{1,0:T(8,128)S(1)} %bitcast.33, f32[4,2,2,128,256]{4,3,2,1,0:T(8,128)S(1)} %bitcast.32, f32[4,256,256]{2,1,0:T(8,128)S(1)} %copy-done), custom_call_target="tpu_custom_call" | custom-call | tf_op jit(solution)/shard_map/pallas_call | solution.py:247
  (20 shorter events, 0.2 us)
Async XLA Ops:
  6.5 29.1 %copy-start = (f32[4,256,256]{2,1,0:T(8,128)S(1)}, f32[4,256,256]{2,1,0:T(8,128)}, u32[]{:S(2)}) copy-start(f32[4,256,256]{2,1,0:T(8,128)} %choi_ref.1) | copy-start | bytes 3145732
  8.6 20.4 %all-to-all-start = ((f32[8,32,256]{2,1,0:T(8,128)}), f32[8,32,256]{2,1,0:T(8,128)S(1)}, u32[]{:S(2)}, u32[]{:S(2)}) async-start(f32[8,32,256]{2,1,0:T(8,128)} %bitcast.6), calls=%async_computation | async-start | bytes 524288 | tf_op jit(solution)/shard_map/all_to_all | solution.py:70
  16.3 75.2 %all-gather.3.cloned.1.call-start = ((), (), s32[]{:S(2)}) async-start(), calls=%async_computation.3 | async-start | bytes 2228224 | tf_op jit(solution)/shard_map/all_gather | solution.py:77
  16.3 18.0 %collective-permute-start = (f32[256,256]{1,0:T(8,128)S(1)}, f32[256,256]{1,0:T(8,128)S(1)}, u32[]{:S(2)}, u32[]{:S(2)}) collective-permute-start(f32[256,256]{1,0:T(8,128)S(1)} %get-tuple-element.21), channel_id=1, source_target_pairs={{0,4},{1,5},{16,20},{17,21},{32,36},{33,37},{48,52},{49,53},{64,68... | collective-permute-start | bytes 786440 | tf_op jit(solution)/shard_map/ppermute | solution.py:34
  22.1 13.5 %collective-permute-start.1 = (f32[256,256]{1,0:T(8,128)S(1)}, f32[256,256]{1,0:T(8,128)S(1)}, u32[]{:S(2)}, u32[]{:S(2)}) collective-permute-start(f32[256,256]{1,0:T(8,128)S(1)} %get-tuple-element.20), channel_id=1, source_target_pairs={{0,8},{1,9},{16,24},{17,25},{32,40},{33,41},{48,56},{49,57},{64,72... | collective-permute-start | bytes 786440 | tf_op jit(solution)/shard_map/ppermute | solution.py:34
  27.7 8.0 %collective-permute-start.2 = (f32[256,256]{1,0:T(8,128)S(1)}, f32[256,256]{1,0:T(8,128)S(1)}, u32[]{:S(2)}, u32[]{:S(2)}) collective-permute-start(f32[256,256]{1,0:T(8,128)S(1)} %get-tuple-element.22), channel_id=1, source_target_pairs={{0,12},{1,13},{16,28},{17,29},{32,44},{33,45},{48,60},{49,61},{64,... | collective-permute-start | bytes 786440 | tf_op jit(solution)/shard_map/ppermute | solution.py:34
  29.0 6.7 %collective-permute-start.3 = (f32[32,256]{1,0:T(8,128)S(1)}, f32[32,256]{1,0:T(8,128)S(1)}, u32[]{:S(2)}, u32[]{:S(2)}) collective-permute-start(f32[32,256]{1,0:T(8,128)S(1)} %slice_bitcast_fusion.3), channel_id=1, source_target_pairs={{0,16},{16,0},{1,17},{17,1},{2,18},{18,2},{3,19},{19,3},{4,20},{20... | collective-permute-start | bytes 98312 | tf_op jit(solution)/shard_map/ppermute | solution.py:52
  32.1 3.6 %collective-permute-start.4 = (f32[32,256]{1,0:T(8,128)S(1)}, f32[32,256]{1,0:T(8,128)S(1)}, u32[]{:S(2)}, u32[]{:S(2)}) collective-permute-start(f32[32,256]{1,0:T(8,128)S(1)} %slice_bitcast_fusion.3), channel_id=1, source_target_pairs={{0,32},{16,48},{1,33},{17,49},{2,34},{18,50},{3,35},{19,51},{4,36}... | collective-permute-start | bytes 98312 | tf_op jit(solution)/shard_map/ppermute | solution.py:53
  34.4 2.3 %collective-permute-start.5 = (f32[32,256]{1,0:T(8,128)S(1)}, f32[32,256]{1,0:T(8,128)S(1)}, u32[]{:S(2)}, u32[]{:S(2)}) collective-permute-start(f32[32,256]{1,0:T(8,128)S(1)} %slice_bitcast_fusion.3), channel_id=1, source_target_pairs={{0,48},{16,32},{1,49},{17,33},{2,50},{18,34},{3,51},{19,35},{4,52}... | collective-permute-start | bytes 98312 | tf_op jit(solution)/shard_map/ppermute | solution.py:54
  36.7 9.6 %collective-permute-start.7 = (f32[64,256]{1,0:T(8,128)S(1)}, f32[64,256]{1,0:T(8,128)S(1)}, u32[]{:S(2)}, u32[]{:S(2)}) collective-permute-start(f32[64,256]{1,0:T(8,128)S(1)} %pad_maximum_fusion.1), channel_id=1, source_target_pairs={{0,8},{1,9},{16,24},{17,25},{32,40},{33,41},{48,56},{49,57},{64,72... | collective-permute-start | bytes 196616 | tf_op jit(solution)/shard_map/ppermute | solution.py:25
  45.0 3.2 %collective-permute-start.6 = (f32[128,256]{1,0:T(8,128)S(1)}, f32[128,256]{1,0:T(8,128)S(1)}, u32[]{:S(2)}, u32[]{:S(2)}) collective-permute-start(f32[128,256]{1,0:T(8,128)S(1)} %split.31), channel_id=1, source_target_pairs={{0,2},{4,6},{8,10},{12,14},{1,3},{5,7},{9,11},{13,15},{16,18},{20,... | collective-permute-start | bytes 393224 | tf_op jit(solution)/shard_map/ppermute | solution.py:41
  49.8 16.2 %all-to-all-start.1 = ((f32[8,64,256]{2,1,0:T(8,128)}), f32[8,64,256]{2,1,0:T(8,128)S(1)}, u32[]{:S(2)}, u32[]{:S(2)}) async-start(f32[8,64,256]{2,1,0:T(8,128)} %broadcast_in_dim.11), calls=%async_computation.1 | async-start | bytes 1048576 | tf_op jit(solution)/shard_map/all_to_all | solution.py:47
  53.3 2.6 %collective-permute-start.8 = (f32[64,256]{1,0:T(8,128)S(1)}, f32[64,256]{1,0:T(8,128)S(1)}, u32[]{:S(2)}, u32[]{:S(2)}) collective-permute-start(f32[64,256]{1,0:T(8,128)S(1)} %broadcast_select_fusion.2), channel_id=1, source_target_pairs={{0,4},{8,12},{1,5},{9,13},{16,20},{24,28},{17,21},{25,29},{32,36},... | collective-permute-start | bytes 196616 | tf_op jit(solution)/shard_map/ppermute | solution.py:25
  55.9 3.2 %collective-permute-start.9 = (f32[64,256]{1,0:T(8,128)S(1)}, f32[64,256]{1,0:T(8,128)S(1)}, u32[]{:S(2)}, u32[]{:S(2)}) collective-permute-start(f32[64,256]{1,0:T(8,128)S(1)} %broadcast_select_fusion.3), channel_id=1, source_target_pairs={{0,2},{4,6},{8,10},{12,14},{1,3},{5,7},{9,11},{13,15},{16,18},{20,... | collective-permute-start | bytes 196616 | tf_op jit(solution)/shard_map/ppermute | solution.py:25
  81.1 9.8 %collective-permute-start.10 = (f32[512,256]{1,0:T(8,128)S(1)}, f32[512,256]{1,0:T(8,128)S(1)}, u32[]{:S(2)}, u32[]{:S(2)}) collective-permute-start(f32[512,256]{1,0:T(8,128)S(1)} %bitcast.34), channel_id=1, source_target_pairs={{0,1},{1,0},{2,3},{3,2},{4,5},{5,4},{6,7},{7,6},{8,9},{9,8},{10,11... | collective-permute-start | bytes 1572872 | tf_op jit(solution)/shard_map/ppermute | solution.py:83
  91.5 1.6 %copy-start.1 = (f32[2048,256]{1,0:T(8,128)S(1)}, f32[2048,256]{1,0:T(8,128)}, u32[]{:S(2)}) copy-start(f32[2048,256]{1,0:T(8,128)} %all-gather.3.cloned.1.call-done) | copy-start | bytes 6291460
Sparse Core Ops, SparseCore 0:
  49.0 42.4 all-gather.2

commit v3 on v2

--- a/solution.py
+++ b/solution.py
@@ -70,13 +70,14 @@
     top = lax.all_to_all(choi[0].reshape(high, tile // high, tile), "y", 0, 0)[0]
     panel = scattered(choi.reshape(slots * tile, tile), "z")
     top = from_two(top)
-    panel, top = together((panel, top))
-    panel = halved(panel, "z")
     lead = doubled(top, "z", 4)
     panel, lead = together((panel, lead))
+    panel = halved(panel, "z")
+    column = gathered(top, "y")
+    lead = doubled(lead, "z", 2)
+    panel, lead = together((panel, lead))
     panels = lax.all_gather(panel, COL)
-    column = gathered(top, "y")
-    lead = doubled(doubled(lead, "z", 2), "z", 1)
+    lead = doubled(lead, "z", 1)
     lead, column = together((lead, column))
     lead = gathered(lead, "y")
     column, half = stacked(column, tile), stacked(lead, tile)

time: 115 us -> 123 us (1.070)
  the two profiles are of different devices: /device:TPU:1 before, /device:TPU:193 now
where the time goes in v3:
time: 123 us
  blocking collectives  37.2 us (30%)
  waiting for transfers between devices  33.3 us (27%)
  starting transfers between devices  18.6 us (15%)
  Pallas kernels  15.1 us (12%)
  between operations  13.7 us (11%)
  local copies, waits for them, and re-layouts  3.92 us (3%)
    all_to_all x1, blocking collectives, gathered(): return lax.all_to_all(copies, axis, 0, 0)  20.2 us
    all_to_all x1, blocking collectives, spread(): lax.all_to_all(choi[0].reshape(high, tile // high, tile), 'y', 0, 0)[0]  17 us
    ppermute x1, waiting for transfers between devices, halved(): sent = lax.ppermute(give, axis, [(i, i + 1) for i in range(0, size, 2)])  15.3 us
    pallas_call x1, Pallas kernels, body(): pl.pallas_call(update_kernel, in_specs=[pl.BlockSpec(memory_space=pltpu.S...  15.1 us
    all_to_all x1, waiting for transfers between devices, gathered(): return lax.all_to_all(copies, axis, 0, 0)  12.6 us
    ppermute x3, waiting for transfers between devices, doubled(): sent = lax.ppermute(block, axis, pairs)  4.01 us
    all_to_all x1, starting transfers between devices, gathered(): return lax.all_to_all(copies, axis, 0, 0)  3.49 us
    ppermute x1, starting transfers between devices, from_two(): near = lax.ppermute(mine, 'x', [(0, 1), (1, 0)])  3.11 us
  transfers between devices with their start and end apart: 13, of which 4 were waited for; matrix products, arithmetic and copies ran while one was open for 1% of the time, Pallas kernels for 0%

profile of v3, /device:TPU:193, one launch (start us, length us, event | category | flops | bytes accessed | tf_op | source)
XLA Modules:
  0.0 123.0 jit_solution(6003813430400480158)
XLA Ops:
  6.5 1.4 %fusion.2 = (f32[1,256,256]{2,1,0:T(8,128)S(1)}, f32[256,256]{1,0:T(8,128)S(1)}, f32[256,256]{1,0:T(8,128)S(1)}, f32[256,256]{1,0:T(8,128)S(1)}) fusion(f32[4,256,256]{2,1,0:T(8,128)} %choi_ref.1), kind=kLoop, calls=%fused_computation.18 | loop fusion | bytes 2097152 | tf_op jit(solution)/shard_map/split | solution.py:31
  7.9 17.0 %all_to_all.15 = f32[8,32,256]{2,1,0:T(8,128)S(1)} all-to-all(f32[8,32,256]{2,1,0:T(8,128)S(1)} %bitcast.37), channel_id=1, replica_groups=mesh['y'=8,'x'=4,'z'=8,'core'=2] {'y'}, dimensions={0} | all-to-all | bytes 524288 | tf_op jit(solution)/shard_map/all_to_all | solution.py:70
  24.9 3.1 %collective-permute-start.3 = (f32[32,256]{1,0:T(8,128)S(1)}, f32[32,256]{1,0:T(8,128)S(1)}, u32[]{:S(2)}, u32[]{:S(2)}) collective-permute-start(f32[32,256]{1,0:T(8,128)S(1)} %slice_bitcast_fusion.3), channel_id=1, source_target_pairs={{0,16},{16,0},{1,17},{17,1},{2,18},{18,2},{3,19},{19,3},{4,20},{20... | collective-permute-start | bytes 98312 | tf_op jit(solution)/shard_map/ppermute | solution.py:52
  28.0 2.2 %collective-permute-start.4 = (f32[32,256]{1,0:T(8,128)S(1)}, f32[32,256]{1,0:T(8,128)S(1)}, u32[]{:S(2)}, u32[]{:S(2)}) collective-permute-start(f32[32,256]{1,0:T(8,128)S(1)} %slice_bitcast_fusion.3), channel_id=1, source_target_pairs={{0,32},{16,48},{1,33},{17,49},{2,34},{18,50},{3,35},{19,51},{4,36}... | collective-permute-start | bytes 98312 | tf_op jit(solution)/shard_map/ppermute | solution.py:53
  30.2 1.3 %collective-permute-start.5 = (f32[32,256]{1,0:T(8,128)S(1)}, f32[32,256]{1,0:T(8,128)S(1)}, u32[]{:S(2)}, u32[]{:S(2)}) collective-permute-start(f32[32,256]{1,0:T(8,128)S(1)} %slice_bitcast_fusion.3), channel_id=1, source_target_pairs={{0,48},{16,32},{1,49},{17,33},{2,50},{18,34},{3,51},{19,35},{4,52}... | collective-permute-start | bytes 98312 | tf_op jit(solution)/shard_map/ppermute | solution.py:54
  31.5 0.7 collective-permute-start
  32.2 0.7 collective-permute-start.1
  32.9 0.0 collective-permute-done.3
  32.9 0.7 collective-permute-start.2
  33.6 0.0 collective-permute-done.4
  33.7 0.7 collective-permute-start.6
  34.4 0.0 collective-permute-done
  34.4 0.1 fusion.1
  34.5 0.7 collective-permute-start.8
  35.2 1.3 %collective-permute-start.7 = (f32[128,256]{1,0:T(8,128)S(1)}, f32[128,256]{1,0:T(8,128)S(1)}, u32[]{:S(2)}, u32[]{:S(2)}) collective-permute-start(f32[128,256]{1,0:T(8,128)S(1)} %split.31), channel_id=1, source_target_pairs={{0,2},{4,6},{8,10},{12,14},{1,3},{5,7},{9,11},{13,15},{16,18},{20,... | collective-permute-start | bytes 393224 | tf_op jit(solution)/shard_map/ppermute | solution.py:41
  36.5 15.3 %collective-permute-done.7 = f32[128,256]{1,0:T(8,128)S(1)} collective-permute-done((f32[128,256]{1,0:T(8,128)S(1)}, f32[128,256]{1,0:T(8,128)S(1)}, u32[]{:S(2)}, u32[]{:S(2)}) %collective-permute-start.7) | collective-permute-done | bytes 131104 | tf_op jit(solution)/shard_map/ppermute | solution.py:41
  51.9 0.7 slice_select_fusion
  52.5 0.0 all-gather.3.cloned.1.call-update
  52.6 0.8 broadcast_in_dim.11
  53.4 3.5 %all-to-all-start.1 = ((f32[8,64,256]{2,1,0:T(8,128)}), f32[8,64,256]{2,1,0:T(8,128)S(1)}, u32[]{:S(2)}, u32[]{:S(2)}) async-start(f32[8,64,256]{2,1,0:T(8,128)} %broadcast_in_dim.11), calls=%async_computation.1 | async-start | bytes 1048576 | tf_op jit(solution)/shard_map/all_to_all | solution.py:47
  56.9 1.3 %collective-permute-start.9 = (f32[64,256]{1,0:T(8,128)S(1)}, f32[64,256]{1,0:T(8,128)S(1)}, u32[]{:S(2)}, u32[]{:S(2)}) collective-permute-start(f32[64,256]{1,0:T(8,128)S(1)} %broadcast_select_fusion.2), channel_id=1, source_target_pairs={{0,2},{4,6},{8,10},{12,14},{1,3},{5,7},{9,11},{13,15},{16,18},{20,... | collective-permute-start | bytes 196616 | tf_op jit(solution)/shard_map/ppermute | solution.py:25
  58.2 4.0 %collective-permute-done.9 = f32[64,256]{1,0:T(8,128)S(1)} collective-permute-done((f32[64,256]{1,0:T(8,128)S(1)}, f32[64,256]{1,0:T(8,128)S(1)}, u32[]{:S(2)}, u32[]{:S(2)}) %collective-permute-start.9) | collective-permute-done | bytes 65568 | tf_op jit(solution)/shard_map/ppermute | solution.py:25
  62.2 12.6 %all-to-all-done.1 = f32[8,64,256]{2,1,0:T(8,128)S(1)} async-done(((f32[8,64,256]{2,1,0:T(8,128)}), f32[8,64,256]{2,1,0:T(8,128)S(1)}, u32[]{:S(2)}, u32[]{:S(2)}) %all-to-all-start.1) | async-done | bytes 524320 | tf_op jit(solution)/shard_map/all_to_all | solution.py:47
  74.8 20.2 %all_to_all.16 = f32[8,64,256]{2,1,0:T(8,128)S(1)} all-to-all(f32[8,64,256]{2,1,0:T(8,128)S(1)} %broadcast_in_dim.12), channel_id=1, replica_groups=mesh['y'=8,'x'=4,'z'=8,'core'=2] {'y'}, dimensions={0} | all-to-all | bytes 1048576 | tf_op jit(solution)/shard_map/all_to_all | solution.py:47
  95.0 2.6 %collective-permute-start.10 = (f32[512,256]{1,0:T(8,128)S(1)}, f32[512,256]{1,0:T(8,128)S(1)}, u32[]{:S(2)}, u32[]{:S(2)}) collective-permute-start(f32[512,256]{1,0:T(8,128)S(1)} %bitcast.34), channel_id=1, source_target_pairs={{0,1},{1,0},{2,3},{3,2},{4,5},{5,4},{6,7},{7,6},{8,9},{9,8},{10,11... | collective-permute-start | bytes 1572872 | tf_op jit(solution)/shard_map/ppermute | solution.py:84
  97.6 0.1 pad_add_fusion.place_ref
  97.8 1.4 %collective-permute-done.10 = f32[512,256]{1,0:T(8,128)S(1)} collective-permute-done((f32[512,256]{1,0:T(8,128)S(1)}, f32[512,256]{1,0:T(8,128)S(1)}, u32[]{:S(2)}, u32[]{:S(2)}) %collective-permute-start.10) | collective-permute-done | bytes 524320 | tf_op jit(solution)/shard_map/ppermute | solution.py:84
  99.1 0.1 broadcast_select_fusion.1
  99.2 0.1 pad_maximum_fusion.lead_ref
  99.4 0.0 all-gather.3.cloned.1.call-done
  99.4 1.6 %copy-done.1 = f32[2048,256]{1,0:T(8,128)S(1)} copy-done((f32[2048,256]{1,0:T(8,128)S(1)}, f32[2048,256]{1,0:T(8,128)}, u32[]{:S(2)}) %copy-start.1) | copy-done | bytes 2097176
  101.0 15.1 %shard_map.17 = f32[4,256,256]{2,1,0:T(8,128)} custom-call(s32[2]{0:T(128)S(1)} %pad_add_fusion.place_ref, f32[512,512]{1,0:T(8,128)S(1)} %pad_maximum_fusion.lead_ref, f32[512,256]{1,0:T(8,128)S(1)} %bitcast.33, f32[4,2,2,128,256]{4,3,2,1,0:T(8,128)S(1)} %bitcast.32, f32[4,256,256]{2,1,0:T(8,128)S(1)} %copy-done), custom_call_target="tpu_custom_call" | custom-call | tf_op jit(solution)/shard_map/pallas_call | solution.py:248
  (19 shorter events, 0.2 us)
Async XLA Ops:
  6.5 27.9 %copy-start = (f32[4,256,256]{2,1,0:T(8,128)S(1)}, f32[4,256,256]{2,1,0:T(8,128)}, u32[]{:S(2)}) copy-start(f32[4,256,256]{2,1,0:T(8,128)} %choi_ref.1) | copy-start | bytes 3145732
  6.5 92.8 %all-gather.3.cloned.1.call-start = ((), (), s32[]{:S(2)}) async-start(), calls=%async_computation.3 | async-start | bytes 2228224 | tf_op jit(solution)/shard_map/all_gather | solution.py:79
  24.9 8.0 %collective-permute-start.3 = (f32[32,256]{1,0:T(8,128)S(1)}, f32[32,256]{1,0:T(8,128)S(1)}, u32[]{:S(2)}, u32[]{:S(2)}) collective-permute-start(f32[32,256]{1,0:T(8,128)S(1)} %slice_bitcast_fusion.3), channel_id=1, source_target_pairs={{0,16},{16,0},{1,17},{17,1},{2,18},{18,2},{3,19},{19,3},{4,20},{20... | collective-permute-start | bytes 98312 | tf_op jit(solution)/shard_map/ppermute | solution.py:52
  28.0 5.6 %collective-permute-start.4 = (f32[32,256]{1,0:T(8,128)S(1)}, f32[32,256]{1,0:T(8,128)S(1)}, u32[]{:S(2)}, u32[]{:S(2)}) collective-permute-start(f32[32,256]{1,0:T(8,128)S(1)} %slice_bitcast_fusion.3), channel_id=1, source_target_pairs={{0,32},{16,48},{1,33},{17,49},{2,34},{18,50},{3,35},{19,51},{4,36}... | collective-permute-start | bytes 98312 | tf_op jit(solution)/shard_map/ppermute | solution.py:53
  30.2 3.4 %collective-permute-start.5 = (f32[32,256]{1,0:T(8,128)S(1)}, f32[32,256]{1,0:T(8,128)S(1)}, u32[]{:S(2)}, u32[]{:S(2)}) collective-permute-start(f32[32,256]{1,0:T(8,128)S(1)} %slice_bitcast_fusion.3), channel_id=1, source_target_pairs={{0,48},{16,32},{1,49},{17,33},{2,50},{18,34},{3,51},{19,35},{4,52}... | collective-permute-start | bytes 98312 | tf_op jit(solution)/shard_map/ppermute | solution.py:54
  31.5 2.8 %collective-permute-start = (f32[256,256]{1,0:T(8,128)S(1)}, f32[256,256]{1,0:T(8,128)S(1)}, u32[]{:S(2)}, u32[]{:S(2)}) collective-permute-start(f32[256,256]{1,0:T(8,128)S(1)} %get-tuple-element.21), channel_id=1, source_target_pairs={{0,4},{1,5},{16,20},{17,21},{32,36},{33,37},{48,52},{49,53},{64,68... | collective-permute-start | bytes 786440 | tf_op jit(solution)/shard_map/ppermute | solution.py:34
  32.2 2.2 %collective-permute-start.1 = (f32[256,256]{1,0:T(8,128)S(1)}, f32[256,256]{1,0:T(8,128)S(1)}, u32[]{:S(2)}, u32[]{:S(2)}) collective-permute-start(f32[256,256]{1,0:T(8,128)S(1)} %get-tuple-element.20), channel_id=1, source_target_pairs={{0,8},{1,9},{16,24},{17,25},{32,40},{33,41},{48,56},{49,57},{64,72... | collective-permute-start | bytes 786440 | tf_op jit(solution)/shard_map/ppermute | solution.py:34
  32.9 1.4 %collective-permute-start.2 = (f32[256,256]{1,0:T(8,128)S(1)}, f32[256,256]{1,0:T(8,128)S(1)}, u32[]{:S(2)}, u32[]{:S(2)}) collective-permute-start(f32[256,256]{1,0:T(8,128)S(1)} %get-tuple-element.22), channel_id=1, source_target_pairs={{0,12},{1,13},{16,28},{17,29},{32,44},{33,45},{48,60},{49,61},{64,... | collective-permute-start | bytes 786440 | tf_op jit(solution)/shard_map/ppermute | solution.py:34
  33.7 0.8 collective-permute-start.6
  34.5 2.0 %collective-permute-start.8 = (f32[64,256]{1,0:T(8,128)S(1)}, f32[64,256]{1,0:T(8,128)S(1)}, u32[]{:S(2)}, u32[]{:S(2)}) collective-permute-start(f32[64,256]{1,0:T(8,128)S(1)} %broadcast_select_fusion.3), channel_id=1, source_target_pairs={{0,4},{8,12},{1,5},{9,13},{16,20},{24,28},{17,21},{25,29},{32,36},... | collective-permute-start | bytes 196616 | tf_op jit(solution)/shard_map/ppermute | solution.py:25
  35.2 16.7 %collective-permute-start.7 = (f32[128,256]{1,0:T(8,128)S(1)}, f32[128,256]{1,0:T(8,128)S(1)}, u32[]{:S(2)}, u32[]{:S(2)}) collective-permute-start(f32[128,256]{1,0:T(8,128)S(1)} %split.31), channel_id=1, source_target_pairs={{0,2},{4,6},{8,10},{12,14},{1,3},{5,7},{9,11},{13,15},{16,18},{20,... | collective-permute-start | bytes 393224 | tf_op jit(solution)/shard_map/ppermute | solution.py:41
  53.4 21.4 %all-to-all-start.1 = ((f32[8,64,256]{2,1,0:T(8,128)}), f32[8,64,256]{2,1,0:T(8,128)S(1)}, u32[]{:S(2)}, u32[]{:S(2)}) async-start(f32[8,64,256]{2,1,0:T(8,128)} %broadcast_in_dim.11), calls=%async_computation.1 | async-start | bytes 1048576 | tf_op jit(solution)/shard_map/all_to_all | solution.py:47
  56.9 5.3 %collective-permute-start.9 = (f32[64,256]{1,0:T(8,128)S(1)}, f32[64,256]{1,0:T(8,128)S(1)}, u32[]{:S(2)}, u32[]{:S(2)}) collective-permute-start(f32[64,256]{1,0:T(8,128)S(1)} %broadcast_select_fusion.2), channel_id=1, source_target_pairs={{0,2},{4,6},{8,10},{12,14},{1,3},{5,7},{9,11},{13,15},{16,18},{20,... | collective-permute-start | bytes 196616 | tf_op jit(solution)/shard_map/ppermute | solution.py:25
  95.0 4.1 %collective-permute-start.10 = (f32[512,256]{1,0:T(8,128)S(1)}, f32[512,256]{1,0:T(8,128)S(1)}, u32[]{:S(2)}, u32[]{:S(2)}) collective-permute-start(f32[512,256]{1,0:T(8,128)S(1)} %bitcast.34), channel_id=1, source_target_pairs={{0,1},{1,0},{2,3},{3,2},{4,5},{5,4},{6,7},{7,6},{8,9},{9,8},{10,11... | collective-permute-start | bytes 1572872 | tf_op jit(solution)/shard_map/ppermute | solution.py:84
  99.4 1.6 %copy-start.1 = (f32[2048,256]{1,0:T(8,128)S(1)}, f32[2048,256]{1,0:T(8,128)}, u32[]{:S(2)}) copy-start(f32[2048,256]{1,0:T(8,128)} %all-gather.3.cloned.1.call-done) | copy-start | bytes 6291460
Sparse Core Ops, SparseCore 0:
  52.7 41.0 all-gather.2

commit v4 on v2

--- a/solution.py
+++ b/solution.py
@@ -30,7 +30,7 @@
     size = lax.axis_size(axis)
     parts = jnp.split(block, size // 2)
     mine = jnp.where(lax.axis_index(axis) == 0, parts[0], 0.0)
-    for i in range(1, size // 2):
+    for i in sorted(range(1, size // 2), key=lambda i: abs(2 * i - size // 2)):
         mine = mine + lax.ppermute(parts[i], axis, [(0, 2 * i)])
     return mine
 

time: 115 us -> 120 us (1.043)
  starting transfers between devices: 51.4 us -> 55.8 us
  waiting for transfers between devices: 14.1 us -> 16.2 us
    all_to_all x1, starting transfers between devices: 3.49 us -> 6.08 us  [gathered(): return lax.all_to_all(copies, axis, 0, 0)]
    all_gather x1, waiting for transfers between devices: 0.41 us -> 2.88 us  [spread(): panels = lax.all_gather(panel, COL)]
    ppermute x1, starting transfers between devices: 8.3 us -> 9.84 us  [spread(): pair = lax.ppermute(half, 'core', [(0, 1), (1, 0)])]
where the time goes in v4:
time: 120 us
  starting transfers between devices  55.8 us (46%)
  waiting for transfers between devices  16.2 us (14%)
  blocking collectives  14.7 us (12%)
  Pallas kernels  13.8 us (12%)
  between operations  13.7 us (11%)
  local copies, waits for them, and re-layouts  4.64 us (4%)
    all_to_all x1, blocking collectives, gathered(): return lax.all_to_all(copies, axis, 0, 0)  14.7 us
    pallas_call x1, Pallas kernels, body(): pl.pallas_call(update_kernel, in_specs=[pl.BlockSpec(memory_space=pltpu.S...  13.8 us
    ppermute x3, starting transfers between devices, scattered(): mine = mine + lax.ppermute(parts[i], axis, [(0, 2 * i)])  13.3 us
    ppermute x3, starting transfers between devices, doubled(): sent = lax.ppermute(block, axis, pairs)  11 us
    ppermute x1, starting transfers between devices, spread(): pair = lax.ppermute(half, 'core', [(0, 1), (1, 0)])  9.84 us
    all_to_all x1, starting transfers between devices, spread(): lax.all_to_all(choi[0].reshape(high, tile // high, tile), 'y', 0, 0)[0]  7.65 us
    all_to_all x1, waiting for transfers between devices, gathered(): return lax.all_to_all(copies, axis, 0, 0)  6.5 us
    all_to_all x1, starting transfers between devices, gathered(): return lax.all_to_all(copies, axis, 0, 0)  6.08 us
  transfers between devices with their start and end apart: 14, of which 7 were waited for; matrix products, arithmetic and copies ran while one was open for 1% of the time, Pallas kernels for 0%

profile of v4, /device:TPU:1, one launch (start us, length us, event | category | flops | bytes accessed | tf_op | source)
XLA Modules:
  0.0 119.9 jit_solution(9140553384058840709)
XLA Ops:
  6.5 2.1 %fusion.2 = (f32[1,256,256]{2,1,0:T(8,128)}, f32[256,256]{1,0:T(8,128)S(1)}, f32[256,256]{1,0:T(8,128)S(1)}, f32[256,256]{1,0:T(8,128)S(1)}) fusion(f32[4,256,256]{2,1,0:T(8,128)} %choi_ref.1), kind=kLoop, calls=%fused_computation.18 | loop fusion | bytes 2097152 | tf_op jit(solution)/shard_map/split | solution.py:31
  8.6 7.7 %all-to-all-start = ((f32[8,32,256]{2,1,0:T(8,128)}), f32[8,32,256]{2,1,0:T(8,128)S(1)}, u32[]{:S(2)}, u32[]{:S(2)}) async-start(f32[8,32,256]{2,1,0:T(8,128)} %bitcast.6), calls=%async_computation | async-start | bytes 524288 | tf_op jit(solution)/shard_map/all_to_all | solution.py:70
  16.3 0.0 all-gather.3.cloned.1.call-start
  16.3 10.6 %collective-permute-start = (f32[256,256]{1,0:T(8,128)S(1)}, f32[256,256]{1,0:T(8,128)S(1)}, u32[]{:S(2)}, u32[]{:S(2)}) collective-permute-start(f32[256,256]{1,0:T(8,128)S(1)} %get-tuple-element.21), channel_id=1, source_target_pairs={{0,8},{1,9},{16,24},{17,25},{32,40},{33,41},{48,56},{49,57},{64,72... | collective-permute-start | bytes 786440 | tf_op jit(solution)/shard_map/ppermute | solution.py:34
  27.0 1.3 %collective-permute-start.1 = (f32[256,256]{1,0:T(8,128)S(1)}, f32[256,256]{1,0:T(8,128)S(1)}, u32[]{:S(2)}, u32[]{:S(2)}) collective-permute-start(f32[256,256]{1,0:T(8,128)S(1)} %get-tuple-element.20), channel_id=1, source_target_pairs={{0,4},{1,5},{16,20},{17,21},{32,36},{33,37},{48,52},{49,53},{64,68... | collective-permute-start | bytes 786440 | tf_op jit(solution)/shard_map/ppermute | solution.py:34
  28.3 1.3 %collective-permute-start.2 = (f32[256,256]{1,0:T(8,128)S(1)}, f32[256,256]{1,0:T(8,128)S(1)}, u32[]{:S(2)}, u32[]{:S(2)}) collective-permute-start(f32[256,256]{1,0:T(8,128)S(1)} %get-tuple-element.22), channel_id=1, source_target_pairs={{0,12},{1,13},{16,28},{17,29},{32,44},{33,45},{48,60},{49,61},{64,... | collective-permute-start | bytes 786440 | tf_op jit(solution)/shard_map/ppermute | solution.py:34
  29.6 3.1 %collective-permute-start.3 = (f32[32,256]{1,0:T(8,128)S(1)}, f32[32,256]{1,0:T(8,128)S(1)}, u32[]{:S(2)}, u32[]{:S(2)}) collective-permute-start(f32[32,256]{1,0:T(8,128)S(1)} %slice_bitcast_fusion.3), channel_id=1, source_target_pairs={{0,16},{16,0},{1,17},{17,1},{2,18},{18,2},{3,19},{19,3},{4,20},{20... | collective-permute-start | bytes 98312 | tf_op jit(solution)/shard_map/ppermute | solution.py:52
  32.8 2.2 %collective-permute-start.4 = (f32[32,256]{1,0:T(8,128)S(1)}, f32[32,256]{1,0:T(8,128)S(1)}, u32[]{:S(2)}, u32[]{:S(2)}) collective-permute-start(f32[32,256]{1,0:T(8,128)S(1)} %slice_bitcast_fusion.3), channel_id=1, source_target_pairs={{0,32},{16,48},{1,33},{17,49},{2,34},{18,50},{3,35},{19,51},{4,36}... | collective-permute-start | bytes 98312 | tf_op jit(solution)/shard_map/ppermute | solution.py:53
  35.0 1.3 %collective-permute-start.5 = (f32[32,256]{1,0:T(8,128)S(1)}, f32[32,256]{1,0:T(8,128)S(1)}, u32[]{:S(2)}, u32[]{:S(2)}) collective-permute-start(f32[32,256]{1,0:T(8,128)S(1)} %slice_bitcast_fusion.3), channel_id=1, source_target_pairs={{0,48},{16,32},{1,49},{17,33},{2,50},{18,34},{3,51},{19,35},{4,52}... | collective-permute-start | bytes 98312 | tf_op jit(solution)/shard_map/ppermute | solution.py:54
  36.3 0.9 collective-permute-done.1
  37.2 0.1 fusion.1
  37.4 7.9 %collective-permute-start.7 = (f32[64,256]{1,0:T(8,128)S(1)}, f32[64,256]{1,0:T(8,128)S(1)}, u32[]{:S(2)}, u32[]{:S(2)}) collective-permute-start(f32[64,256]{1,0:T(8,128)S(1)} %pad_maximum_fusion.1), channel_id=1, source_target_pairs={{0,8},{1,9},{16,24},{17,25},{32,40},{33,41},{48,56},{49,57},{64,72... | collective-permute-start | bytes 196616 | tf_op jit(solution)/shard_map/ppermute | solution.py:25
  45.3 1.3 %collective-permute-start.6 = (f32[128,256]{1,0:T(8,128)S(1)}, f32[128,256]{1,0:T(8,128)S(1)}, u32[]{:S(2)}, u32[]{:S(2)}) collective-permute-start(f32[128,256]{1,0:T(8,128)S(1)} %split.31), channel_id=1, source_target_pairs={{0,2},{4,6},{8,10},{12,14},{1,3},{5,7},{9,11},{13,15},{16,18},{20,... | collective-permute-start | bytes 393224 | tf_op jit(solution)/shard_map/ppermute | solution.py:41
  46.6 1.9 %collective-permute-done.6 = f32[128,256]{1,0:T(8,128)S(1)} collective-permute-done((f32[128,256]{1,0:T(8,128)S(1)}, f32[128,256]{1,0:T(8,128)S(1)}, u32[]{:S(2)}, u32[]{:S(2)}) %collective-permute-start.6) | collective-permute-done | bytes 131104 | tf_op jit(solution)/shard_map/ppermute | solution.py:41
  48.5 0.7 slice_select_fusion
  49.2 0.0 all-gather.3.cloned.1.call-update
  49.2 0.8 broadcast_in_dim.11
  50.1 6.1 %all-to-all-start.1 = ((f32[8,64,256]{2,1,0:T(8,128)}), f32[8,64,256]{2,1,0:T(8,128)S(1)}, u32[]{:S(2)}, u32[]{:S(2)}) async-start(f32[8,64,256]{2,1,0:T(8,128)} %broadcast_in_dim.11), calls=%async_computation.1 | async-start | bytes 1048576 | tf_op jit(solution)/shard_map/all_to_all | solution.py:47
  56.1 1.3 %collective-permute-start.8 = (f32[64,256]{1,0:T(8,128)S(1)}, f32[64,256]{1,0:T(8,128)S(1)}, u32[]{:S(2)}, u32[]{:S(2)}) collective-permute-start(f32[64,256]{1,0:T(8,128)S(1)} %broadcast_select_fusion.2), channel_id=1, source_target_pairs={{0,4},{8,12},{1,5},{9,13},{16,20},{24,28},{17,21},{25,29},{32,36},... | collective-permute-start | bytes 196616 | tf_op jit(solution)/shard_map/ppermute | solution.py:25
  57.4 1.3 %collective-permute-done.8 = f32[64,256]{1,0:T(8,128)S(1)} collective-permute-done((f32[64,256]{1,0:T(8,128)S(1)}, f32[64,256]{1,0:T(8,128)S(1)}, u32[]{:S(2)}, u32[]{:S(2)}) %collective-permute-start.8) | collective-permute-done | bytes 65568 | tf_op jit(solution)/shard_map/ppermute | solution.py:25
  58.7 1.9 %collective-permute-start.9 = (f32[64,256]{1,0:T(8,128)S(1)}, f32[64,256]{1,0:T(8,128)S(1)}, u32[]{:S(2)}, u32[]{:S(2)}) collective-permute-start(f32[64,256]{1,0:T(8,128)S(1)} %broadcast_select_fusion.3), channel_id=1, source_target_pairs={{0,2},{4,6},{8,10},{12,14},{1,3},{5,7},{9,11},{13,15},{16,18},{20,... | collective-permute-start | bytes 196616 | tf_op jit(solution)/shard_map/ppermute | solution.py:25
  60.6 1.3 %collective-permute-done.9 = f32[64,256]{1,0:T(8,128)S(1)} collective-permute-done((f32[64,256]{1,0:T(8,128)S(1)}, f32[64,256]{1,0:T(8,128)S(1)}, u32[]{:S(2)}, u32[]{:S(2)}) %collective-permute-start.9) | collective-permute-done | bytes 65568 | tf_op jit(solution)/shard_map/ppermute | solution.py:25
  61.9 6.5 %all-to-all-done.1 = f32[8,64,256]{2,1,0:T(8,128)S(1)} async-done(((f32[8,64,256]{2,1,0:T(8,128)}), f32[8,64,256]{2,1,0:T(8,128)S(1)}, u32[]{:S(2)}, u32[]{:S(2)}) %all-to-all-start.1) | async-done | bytes 524320 | tf_op jit(solution)/shard_map/all_to_all | solution.py:47
  68.5 14.7 %all_to_all.15 = f32[8,64,256]{2,1,0:T(8,128)S(1)} all-to-all(f32[8,64,256]{2,1,0:T(8,128)S(1)} %broadcast_in_dim.12), channel_id=1, replica_groups=mesh['y'=8,'x'=4,'z'=8,'core'=2] {'y'}, dimensions={0} | all-to-all | bytes 1048576 | tf_op jit(solution)/shard_map/all_to_all | solution.py:47
  83.2 9.8 %collective-permute-start.10 = (f32[512,256]{1,0:T(8,128)S(1)}, f32[512,256]{1,0:T(8,128)S(1)}, u32[]{:S(2)}, u32[]{:S(2)}) collective-permute-start(f32[512,256]{1,0:T(8,128)S(1)} %bitcast.34), channel_id=1, source_target_pairs={{0,1},{1,0},{2,3},{3,2},{4,5},{5,4},{6,7},{7,6},{8,9},{9,8},{10,11... | collective-permute-start | bytes 1572872 | tf_op jit(solution)/shard_map/ppermute | solution.py:83
  93.0 0.1 pad_add_fusion.place_ref
  93.2 1.4 %collective-permute-done.10 = f32[512,256]{1,0:T(8,128)S(1)} collective-permute-done((f32[512,256]{1,0:T(8,128)S(1)}, f32[512,256]{1,0:T(8,128)S(1)}, u32[]{:S(2)}, u32[]{:S(2)}) %collective-permute-start.10) | collective-permute-done | bytes 524320 | tf_op jit(solution)/shard_map/ppermute | solution.py:83
  94.5 0.1 broadcast_select_fusion.1
  94.6 0.1 pad_maximum_fusion.lead_ref
  94.8 2.9 %all-gather.3.cloned.1.call-done = f32[2048,256]{1,0:T(8,128)} async-done(((f32[128,256]{1,0:T(8,128)}), f32[2048,256]{1,0:T(8,128)}) %all-gather.3.cloned.1.call-update) | async-done | bytes 2097168 | tf_op jit(solution)/shard_map/all_gather | solution.py:77
  97.7 1.6 %copy-done.1 = f32[2048,256]{1,0:T(8,128)S(1)} copy-done((f32[2048,256]{1,0:T(8,128)S(1)}, f32[2048,256]{1,0:T(8,128)}, u32[]{:S(2)}) %copy-start.1) | copy-done | bytes 2097176
  99.2 13.8 %shard_map.17 = f32[4,256,256]{2,1,0:T(8,128)} custom-call(s32[2]{0:T(128)S(1)} %pad_add_fusion.place_ref, f32[512,512]{1,0:T(8,128)S(1)} %pad_maximum_fusion.lead_ref, f32[512,256]{1,0:T(8,128)S(1)} %bitcast.33, f32[4,2,2,128,256]{4,3,2,1,0:T(8,128)S(1)} %bitcast.32, f32[4,256,256]{2,1,0:T(8,128)S(1)} %copy-done), custom_call_target="tpu_custom_call" | custom-call | tf_op jit(solution)/shard_map/pallas_call | solution.py:247
  (20 shorter events, 0.2 us)
Async XLA Ops:
  6.5 30.7 %copy-start = (f32[4,256,256]{2,1,0:T(8,128)S(1)}, f32[4,256,256]{2,1,0:T(8,128)}, u32[]{:S(2)}) copy-start(f32[4,256,256]{2,1,0:T(8,128)} %choi_ref.1) | copy-start | bytes 3145732
  8.6 21.0 %all-to-all-start = ((f32[8,32,256]{2,1,0:T(8,128)}), f32[8,32,256]{2,1,0:T(8,128)S(1)}, u32[]{:S(2)}, u32[]{:S(2)}) async-start(f32[8,32,256]{2,1,0:T(8,128)} %bitcast.6), calls=%async_computation | async-start | bytes 524288 | tf_op jit(solution)/shard_map/all_to_all | solution.py:70
  16.3 81.4 %all-gather.3.cloned.1.call-start = ((), (), s32[]{:S(2)}) async-start(), calls=%async_computation.3 | async-start | bytes 2228224 | tf_op jit(solution)/shard_map/all_gather | solution.py:77
  16.3 18.7 %collective-permute-start = (f32[256,256]{1,0:T(8,128)S(1)}, f32[256,256]{1,0:T(8,128)S(1)}, u32[]{:S(2)}, u32[]{:S(2)}) collective-permute-start(f32[256,256]{1,0:T(8,128)S(1)} %get-tuple-element.21), channel_id=1, source_target_pairs={{0,8},{1,9},{16,24},{17,25},{32,40},{33,41},{48,56},{49,57},{64,72... | collective-permute-start | bytes 786440 | tf_op jit(solution)/shard_map/ppermute | solution.py:34
  27.0 10.2 %collective-permute-start.1 = (f32[256,256]{1,0:T(8,128)S(1)}, f32[256,256]{1,0:T(8,128)S(1)}, u32[]{:S(2)}, u32[]{:S(2)}) collective-permute-start(f32[256,256]{1,0:T(8,128)S(1)} %get-tuple-element.20), channel_id=1, source_target_pairs={{0,4},{1,5},{16,20},{17,21},{32,36},{33,37},{48,52},{49,53},{64,68... | collective-permute-start | bytes 786440 | tf_op jit(solution)/shard_map/ppermute | solution.py:34
  28.3 8.9 %collective-permute-start.2 = (f32[256,256]{1,0:T(8,128)S(1)}, f32[256,256]{1,0:T(8,128)S(1)}, u32[]{:S(2)}, u32[]{:S(2)}) collective-permute-start(f32[256,256]{1,0:T(8,128)S(1)} %get-tuple-element.22), channel_id=1, source_target_pairs={{0,12},{1,13},{16,28},{17,29},{32,44},{33,45},{48,60},{49,61},{64,... | collective-permute-start | bytes 786440 | tf_op jit(solution)/shard_map/ppermute | solution.py:34
  29.6 7.7 %collective-permute-start.3 = (f32[32,256]{1,0:T(8,128)S(1)}, f32[32,256]{1,0:T(8,128)S(1)}, u32[]{:S(2)}, u32[]{:S(2)}) collective-permute-start(f32[32,256]{1,0:T(8,128)S(1)} %slice_bitcast_fusion.3), channel_id=1, source_target_pairs={{0,16},{16,0},{1,17},{17,1},{2,18},{18,2},{3,19},{19,3},{4,20},{20... | collective-permute-start | bytes 98312 | tf_op jit(solution)/shard_map/ppermute | solution.py:52
  32.8 4.5 %collective-permute-start.4 = (f32[32,256]{1,0:T(8,128)S(1)}, f32[32,256]{1,0:T(8,128)S(1)}, u32[]{:S(2)}, u32[]{:S(2)}) collective-permute-start(f32[32,256]{1,0:T(8,128)S(1)} %slice_bitcast_fusion.3), channel_id=1, source_target_pairs={{0,32},{16,48},{1,33},{17,49},{2,34},{18,50},{3,35},{19,51},{4,36}... | collective-permute-start | bytes 98312 | tf_op jit(solution)/shard_map/ppermute | solution.py:53
  35.0 2.3 %collective-permute-start.5 = (f32[32,256]{1,0:T(8,128)S(1)}, f32[32,256]{1,0:T(8,128)S(1)}, u32[]{:S(2)}, u32[]{:S(2)}) collective-permute-start(f32[32,256]{1,0:T(8,128)S(1)} %slice_bitcast_fusion.3), channel_id=1, source_target_pairs={{0,48},{16,32},{1,49},{17,33},{2,50},{18,34},{3,51},{19,35},{4,52}... | collective-permute-start | bytes 98312 | tf_op jit(solution)/shard_map/ppermute | solution.py:54
  37.4 9.2 %collective-permute-start.7 = (f32[64,256]{1,0:T(8,128)S(1)}, f32[64,256]{1,0:T(8,128)S(1)}, u32[]{:S(2)}, u32[]{:S(2)}) collective-permute-start(f32[64,256]{1,0:T(8,128)S(1)} %pad_maximum_fusion.1), channel_id=1, source_target_pairs={{0,8},{1,9},{16,24},{17,25},{32,40},{33,41},{48,56},{49,57},{64,72... | collective-permute-start | bytes 196616 | tf_op jit(solution)/shard_map/ppermute | solution.py:25
  45.3 3.2 %collective-permute-start.6 = (f32[128,256]{1,0:T(8,128)S(1)}, f32[128,256]{1,0:T(8,128)S(1)}, u32[]{:S(2)}, u32[]{:S(2)}) collective-permute-start(f32[128,256]{1,0:T(8,128)S(1)} %split.31), channel_id=1, source_target_pairs={{0,2},{4,6},{8,10},{12,14},{1,3},{5,7},{9,11},{13,15},{16,18},{20,... | collective-permute-start | bytes 393224 | tf_op jit(solution)/shard_map/ppermute | solution.py:41
  50.1 18.4 %all-to-all-start.1 = ((f32[8,64,256]{2,1,0:T(8,128)}), f32[8,64,256]{2,1,0:T(8,128)S(1)}, u32[]{:S(2)}, u32[]{:S(2)}) async-start(f32[8,64,256]{2,1,0:T(8,128)} %broadcast_in_dim.11), calls=%async_computation.1 | async-start | bytes 1048576 | tf_op jit(solution)/shard_map/all_to_all | solution.py:47
  56.1 2.6 %collective-permute-start.8 = (f32[64,256]{1,0:T(8,128)S(1)}, f32[64,256]{1,0:T(8,128)S(1)}, u32[]{:S(2)}, u32[]{:S(2)}) collective-permute-start(f32[64,256]{1,0:T(8,128)S(1)} %broadcast_select_fusion.2), channel_id=1, source_target_pairs={{0,4},{8,12},{1,5},{9,13},{16,20},{24,28},{17,21},{25,29},{32,36},... | collective-permute-start | bytes 196616 | tf_op jit(solution)/shard_map/ppermute | solution.py:25
  58.7 3.2 %collective-permute-start.9 = (f32[64,256]{1,0:T(8,128)S(1)}, f32[64,256]{1,0:T(8,128)S(1)}, u32[]{:S(2)}, u32[]{:S(2)}) collective-permute-start(f32[64,256]{1,0:T(8,128)S(1)} %broadcast_select_fusion.3), channel_id=1, source_target_pairs={{0,2},{4,6},{8,10},{12,14},{1,3},{5,7},{9,11},{13,15},{16,18},{20,... | collective-permute-start | bytes 196616 | tf_op jit(solution)/shard_map/ppermute | solution.py:25
  83.2 11.4 %collective-permute-start.10 = (f32[512,256]{1,0:T(8,128)S(1)}, f32[512,256]{1,0:T(8,128)S(1)}, u32[]{:S(2)}, u32[]{:S(2)}) collective-permute-start(f32[512,256]{1,0:T(8,128)S(1)} %bitcast.34), channel_id=1, source_target_pairs={{0,1},{1,0},{2,3},{3,2},{4,5},{5,4},{6,7},{7,6},{8,9},{9,8},{10,11... | collective-permute-start | bytes 1572872 | tf_op jit(solution)/shard_map/ppermute | solution.py:83
  97.7 1.6 %copy-start.1 = (f32[2048,256]{1,0:T(8,128)S(1)}, f32[2048,256]{1,0:T(8,128)}, u32[]{:S(2)}) copy-start(f32[2048,256]{1,0:T(8,128)} %all-gather.3.cloned.1.call-done) | copy-start | bytes 6291460
Sparse Core Ops, SparseCore 0:
  49.3 48.2 all-gather.2
